TPU v7x, 512 devices: a whole 4x4x16 slice. The times are simulated.
512 devices in a mesh: dp: 16 (over x, y), tile: 32 (over z, core).
Axes of the slice: x: 4, y: 4, z: 16, core: 2. Of those that a mesh axis runs over, the one named last changes fastest.
Arguments:
- calibration: bfloat16 [2048, 32768], P('dp', 'tile'), may hold values from -72 to 72
- sketch: bfloat16 [32768, 256], P('tile'), may hold values from -6 to 6
- weights: bfloat16 [16384, 32768], P(('dp', 'tile')), may hold values from -6 to 6
- tile_ranks: int32 [16, 32], P('dp', 'tile'), may hold values from 32 to 256
Outputs:
- basis_factor: bfloat16 [16384, 8192], P(('dp', 'tile'))
- coefficients: bfloat16 [4096, 32768], P('dp', 'tile')
All inputs are finite; a program needn't handle non-finite values.
Results may differ from a plain program's by a relative error of at most 0.007.
Values may be sent and summed in bfloat16 or wider, within the bound.
No kernel may reach another device: no remote copies, remote signals or barrier semaphores. Data moves between devices by JAX's collectives and lax.ppermute only.
A program may use at most 128 MiB of HBM per device.

v0:
```python
import functools
import math

import jax
import jax.numpy as jnp
from jax import lax
from jax.experimental import pallas as pl
from jax.experimental.pallas import tpu as pltpu
from jax.sharding import PartitionSpec as P

DAMPING = 0.1
NB = 128
STRIP = 8
F32 = jnp.float32
BF16 = jnp.bfloat16

NT = (((1,), (1,)), ((), ()))
NN = (((1,), (0,)), ((), ()))


def dot(a, b, dims):
    return lax.dot_general(a, b, dims, preferred_element_type=F32)


def split2(x):
    hi = x.astype(BF16)
    lo = (x - hi.astype(F32)).astype(BF16)
    return hi, lo


def split3(x):
    hi = x.astype(BF16)
    rest = x - hi.astype(F32)
    mid = rest.astype(BF16)
    lo = (rest - mid.astype(F32)).astype(BF16)
    return hi, mid, lo


def dot3(a, b, dims):
    ah, al = split2(a)
    bh, bl = split2(b)
    return dot(ah, bh, dims) + (dot(ah, bl, dims) + dot(al, bh, dims))


def dot6(a, b, dims):
    ah, am, al = split3(a)
    bh, bm, bl = split3(b)
    small = dot(am, bm, dims) + (dot(ah, bl, dims) + dot(al, bh, dims))
    return dot(ah, bh, dims) + ((dot(ah, bm, dims) + dot(am, bh, dims)) + small)


def inverse_factor(rows):
    shape = rows[0].shape
    lane = lax.broadcasted_iota(jnp.int32, shape, 1)
    sub = lax.broadcasted_iota(jnp.int32, shape, 0)
    rows = list(rows)
    out = []

    def columns(strip, base):
        return [jnp.broadcast_to(strip[:, base + k : base + k + 1], shape) for k in range(STRIP)]

    for s in range(len(rows)):
        base = s * STRIP
        strip = rows[s]
        last = s + 1 == len(rows)
        cols = columns(strip, base)
        a = [
            [jnp.broadcast_to(cols[k][i : i + 1, :], shape) if i >= k else None for k in range(STRIP)]
            for i in range(STRIP)
        ]
        own = (lane >= base) & (lane < base + STRIP)
        held = jnp.where(own, jnp.where(lane - base == sub, 1.0, 0.0), strip)
        y = [jnp.broadcast_to(held[k : k + 1, :], shape) for k in range(STRIP)]
        if not last:
            below = columns(rows[s + 1], base)
            near = jnp.where(own, 0.0, rows[s + 1])
        z = []
        low = [[None] * STRIP for _ in range(STRIP)]
        done = jnp.zeros(shape, F32)
        for k in range(STRIP):
            r = pl.reciprocal(a[k][k], approx=True)
            for i in range(k + 1, STRIP):
                low[i][k] = a[i][k] * r
                for j in range(k + 1, i + 1):
                    a[i][j] = a[i][j] - low[i][k] * a[j][k]
            for i in range(k + 1, STRIP):
                y[i] = y[i] - low[i][k] * y[k]
            if not last:
                low_near = below[k] * r
                for j in range(k + 1, STRIP):
                    below[j] = below[j] - low_near * a[j][k]
                near = near - low_near * y[k]
            z.append(y[k] * r)
            done = jnp.where(sub == k, y[k] * lax.rsqrt(a[k][k]), done)
        out.append(jnp.where(lane < base + STRIP, done, 0.0))
        if last:
            break
        rows[s + 1] = near
        for k in range(STRIP - 1, -1, -1):
            for i in range(k):
                z[i] = z[i] - low[k][i] * z[k]
        for t in range(s + 2, len(rows)):
            taken = columns(rows[t], base)
            total = jnp.where(own, 0.0, rows[t])
            for k in range(STRIP - 1, -1, -1):
                total = total - taken[k] * z[k]
            rows[t] = total
    return out


def factor_into(strips, inv_ref):
    for s, rows in enumerate(inverse_factor(strips)):
        inv_ref[s * STRIP : (s + 1) * STRIP, :] = rows


def prepare_kernel(x_ref, w_ref, high_ref, low_ref, pieces_ref, sems):
    pieces, _, width = pieces_ref.shape
    copies = [
        pltpu.make_async_copy(w_ref.at[:, pl.ds(t * width, width)], pieces_ref.at[t], sems.at[t]) for t in range(pieces)
    ]
    for copy in copies:
        copy.start()
    half = high_ref.shape[0]
    high_ref[...] = x_ref[:, :half].T
    low_ref[...] = x_ref[:, half:].T
    for copy in copies:
        copy.wait()


def prepare(x, weights):
    tokens, width = x.shape
    rows, columns = weights.shape
    pieces = columns // width
    half = jax.ShapeDtypeStruct((width // 2, tokens), x.dtype)
    return pl.pallas_call(
        prepare_kernel,
        out_shape=(half, half, jax.ShapeDtypeStruct((pieces, rows, width), weights.dtype)),
        in_specs=[pl.BlockSpec(memory_space=pltpu.VMEM), pl.BlockSpec(memory_space=pltpu.HBM)],
        out_specs=(pl.BlockSpec(memory_space=pltpu.VMEM),) * 3,
        scratch_shapes=[pltpu.SemaphoreType.DMA((pieces,))],
        compiler_params=pltpu.CompilerParams(vmem_limit_bytes=16 * 1024 * 1024),
    )(x, weights)


def shifted(value, axis, shift):
    side = lax.axis_size(axis)
    return lax.ppermute(value, axis, [(i, (i + shift) % side) for i in range(side)])


FAR_FIRST = (2, 1, -1)


def gather_plane(high, low):
    lines = [tuple(shifted(half, axis, d) for d in FAR_FIRST) for half, axis in ((high, "x"), (low, "y"))]
    lines = lax.optimization_barrier(lines)
    lines = [jnp.stack((half,) + line) for half, line in zip((high, low), lines)]
    return [(line,) + tuple(shifted(line, axis, d) for d in FAR_FIRST) for line, axis in zip(lines, ("y", "x"))]


def whiten_kernel(*refs):
    first, second = refs[:4], refs[4:8]
    sketch_ref, out_ref, a_ref, d_ref, inv_ref, acc_ref = refs[8:]
    outer = len(first)
    inner, half, _ = first[0].shape
    width = 2 * half
    panels = width // NB
    wide = 2 * NB

    def pair(x, y, upper):
        parts = [first[y][x + d] if upper else second[x + d][y] for d in range(2)]
        return jnp.concatenate(parts, axis=1)

    for c in range(panels // 2):
        lo = c * wide
        top = bottom = None
        for x in range(0, inner, 2):
            for y in range(outer):
                low_part = pair(x, y, False)
                if lo < half:
                    high_part = pair(x, y, True)
                    right = high_part[lo : lo + wide, :]
                    term = dot(high_part[lo:, :], right, NT)
                    top = term if top is None else top + term
                    term = dot(low_part, right, NT)
                else:
                    at = lo - half
                    term = dot(low_part[at:, :], low_part[at : at + wide, :], NT)
                bottom = term if bottom is None else bottom + term
        if lo < half:
            a_ref[2 * c, lo:half, :] = top[:, :NB]
            a_ref[2 * c + 1, lo:half, :] = top[:, NB:]
        from_row = max(lo, half)
        a_ref[2 * c, from_row:, :] = bottom[:, :NB]
        a_ref[2 * c + 1, from_row:, :] = bottom[:, NB:]

    lane = lax.broadcasted_iota(jnp.int32, (NB, NB), 1)
    sub = lax.broadcasted_iota(jnp.int32, (NB, NB), 0)
    diag = lane == sub
    trace = jnp.zeros((NB, NB), F32)
    for c in range(panels):
        trace = trace + jnp.where(diag, a_ref[c, c * NB : (c + 1) * NB, :], 0.0)
    damp = jnp.sum(trace) * (DAMPING / width)
    for c in range(panels):
        block = a_ref[c, c * NB : (c + 1) * NB, :]
        a_ref[c, c * NB : (c + 1) * NB, :] = jnp.where(diag, block + damp, block)

    inv_ref[...] = jnp.zeros_like(inv_ref)
    acc_ref[...] = jnp.zeros_like(acc_ref)
    d_ref[...] = a_ref[0, :NB, :]

    tall_row = lax.broadcasted_iota(jnp.int32, (width, NB), 0)
    tall_lane = lax.broadcasted_iota(jnp.int32, (width, NB), 1)

    def panel_of(p, inv):
        ih, il = split2(inv)
        ph, pm = split2(a_ref[p])
        panel = dot(jnp.concatenate([ph, pm], axis=1), jnp.concatenate([ih, ih], axis=1), NT) + dot(ph, il, NT)
        return jnp.where(tall_row >= tall_lane + p * NB, panel, 0.0)

    def sketch_in(p, both):
        part = sketch_ref[p]
        acc_ref[...] += dot(jnp.concatenate([part, part], axis=1), both, NT)

    def step(p, carry):
        strips = [d_ref[s * STRIP : (s + 1) * STRIP, :] for s in range(NB // STRIP)]
        before = jnp.maximum(p - 1, 0)
        panel = panel_of(before, inv_ref[...])
        hi, lo16 = split2(panel)
        both = jnp.concatenate([hi, lo16], axis=1)
        right = tall_row >= p * NB
        hi_r = jnp.where(right, panel, 0.0).astype(BF16)
        lo_r = jnp.where(right, panel - hi.astype(F32), 0.0).astype(BF16)
        twice = jnp.concatenate([hi_r, hi_r], axis=1)
        for c in range(panels // 2):
            lo = c * wide
            off = dot(both[lo:], twice[lo : lo + wide], NT) + dot(hi[lo:], lo_r[lo : lo + wide], NT)
            a_ref[2 * c, lo:, :] -= off[:, :NB]
            a_ref[2 * c + 1, lo:, :] -= off[:, NB:]
        sketch_in(before, both)
        factor_into(strips, inv_ref)
        nxt = jnp.minimum(p + 1, panels - 1)
        rows_n = pl.ds(pl.multiple_of(nxt * NB, NB), NB)
        near = dot3(a_ref[p, rows_n, :], inv_ref[...], NT)
        d_ref[...] = a_ref[nxt, rows_n, :] - dot3(near, near, NT)
        return carry

    lax.fori_loop(0, panels, step, 0)
    hi, lo16 = split2(panel_of(panels - 1, inv_ref[...]))
    sketch_in(panels - 1, jnp.concatenate([hi, lo16], axis=1))
    out_ref[...] = acc_ref[...].astype(BF16)


def whiten(first, second, sketch_t):
    width = 2 * first[0].shape[1]
    panels, rmax, _ = sketch_t.shape
    return pl.pallas_call(
        whiten_kernel,
        out_shape=jax.ShapeDtypeStruct((rmax, width), BF16),
        in_specs=[pl.BlockSpec(memory_space=pltpu.VMEM)] * 9,
        out_specs=pl.BlockSpec(memory_space=pltpu.VMEM),
        scratch_shapes=[
            pltpu.VMEM((panels, width, NB), F32),
            pltpu.VMEM((NB, NB), F32),
            pltpu.VMEM((NB, NB), F32),
            pltpu.VMEM((rmax, width), F32),
        ],
        compiler_params=pltpu.CompilerParams(vmem_limit_bytes=24 * 1024 * 1024),
    )(*first, *second, sketch_t)


def basis_kernel(rank_ref, w_ref, sk_ref, turned_ref, basis_ref, first_inv, second_inv):
    width = w_ref.shape[0]
    rmax = sk_ref.shape[0]
    rank = rank_ref[0, 0]
    kept = lax.broadcasted_iota(jnp.int32, sk_ref.shape, 0) < rank
    masked = jnp.where(kept, sk_ref[...].astype(F32), 0.0).astype(BF16)
    rows = dot(masked, w_ref[...], NT)
    inner = dot6(rows, rows, NT)
    sub = lax.broadcasted_iota(jnp.int32, (rmax, rmax), 0)
    lane = lax.broadcasted_iota(jnp.int32, (rmax, rmax), 1)
    inner = inner + jnp.where((sub == lane) & (sub >= rank), 1.0, 0.0)
    inv_ref = (first_inv, second_inv)

    def factor(block, p):
        factor_into([block[s * STRIP : (s + 1) * STRIP] for s in range(NB // STRIP)], inv_ref[p])
        return inv_ref[p][...]

    def put(base, p):
        scaled = base * math.sqrt(width)
        turned_ref[p * NB : (p + 1) * NB, :] = scaled.astype(BF16)
        basis_ref[:, p * NB : (p + 1) * NB] = scaled.T.astype(BF16)

    inv = factor(inner[:NB, :NB], 0)
    low = dot6(inner[NB:, :NB], inv, NT)
    rest = inner[NB:, NB:] - dot6(low, low, NT)
    base = dot3(inv, rows[:NB], NN)
    left = rows[NB:] - dot3(low, base, NN)
    put(base, 0)
    put(dot3(factor(rest, 1), left, NN), 1)


def basis_of(rank, tile_block, sketched_t):
    width = tile_block.shape[0]
    rmax = sketched_t.shape[0]
    return pl.pallas_call(
        basis_kernel,
        out_shape=(
            jax.ShapeDtypeStruct((rmax, width), BF16),
            jax.ShapeDtypeStruct((width, rmax), BF16),
        ),
        in_specs=[
            pl.BlockSpec(memory_space=pltpu.SMEM),
            pl.BlockSpec(memory_space=pltpu.VMEM),
            pl.BlockSpec(memory_space=pltpu.VMEM),
        ],
        out_specs=(pl.BlockSpec(memory_space=pltpu.VMEM),) * 2,
        scratch_shapes=[
            pltpu.VMEM((NB, NB), F32),
            pltpu.VMEM((NB, NB), F32),
        ],
        compiler_params=pltpu.CompilerParams(vmem_limit_bytes=24 * 1024 * 1024),
    )(rank, tile_block, sketched_t)


def local(calibration, sketch, weights, tile_ranks):
    width = calibration.shape[1]
    rmax = sketch.shape[1]
    high, low, pieces = prepare(calibration, weights)
    tile_block = lax.all_to_all(pieces, "tile", split_axis=0, concat_axis=0, tiled=True).reshape(width, width)
    first, second = gather_plane(high, low)
    sketch_t = sketch.reshape(width // NB, NB, rmax).transpose(0, 2, 1)
    sketched_t = whiten(first, second, sketch_t)
    turned, basis = basis_of(tile_ranks, tile_block, sketched_t)
    served = lax.all_to_all(basis, "tile", split_axis=0, concat_axis=1, tiled=True)
    coeffs = jnp.dot(turned, tile_block, preferred_element_type=F32) / math.sqrt(width)
    return (served, coeffs.astype(BF16))


def solution(mesh):
    tokens, tiles = mesh.devices.shape
    side = math.isqrt(tokens)
    plane = jax.sharding.Mesh(mesh.devices.reshape(side, side, tiles), ("x", "y", "tile"))
    dp = ("x", "y")
    return jax.shard_map(
        local,
        mesh=plane,
        in_specs=(P(dp, "tile"), P("tile", None), P((*dp, "tile"), None), P(dp, "tile")),
        out_specs=(P((*dp, "tile"), None), P(dp, "tile")),
        check_vma=False,
    )
```

profile of v0, /device:TPU:1, one launch (start us, length us, event | category | flops | bytes accessed | tf_op | source)
XLA Modules:
  0.0 198.7 jit_solution(325620878526095338)
XLA Ops:
  0.6 1.6 copy-done.1
  2.2 0.9 copy-done.7
  3.2 1.1 shard_map.59
  4.3 1.3 copy-done.2
  5.6 16.7 %all-to-all-start = ((bf16[32,32,1024]{2,1,0:T(8,128)(2,1)}), bf16[32,32,1024]{2,1,0:T(8,128)(2,1)S(1)}, u32[]{:S(2)}, u32[]{:S(2)}) async-start(bf16[32,32,1024]{2,1,0:T(8,128)(2,1)} %copy-done.2), calls=%async_computation | async-start | bytes 4194304 | tf_op jit(solution)/shard_map/all_to_all | solution.py:329
  22.4 4.7 %collective-permute-start = (bf16[512,128]{1,0:T(8,128)(2,1)S(1)}, bf16[512,128]{1,0:T(8,128)(2,1)S(1)}, u32[]{:S(2)}, u32[]{:S(2)}) collective-permute-start(bf16[512,128]{1,0:T(8,128)(2,1)S(1)} %get-tuple-element.14), channel_id=1, source_target_pairs={{0,256},{128,384},{256,0},{384,128},{1,257},{129,385},{257,1},{385... | collective-permute-start | bytes 393224 | tf_op jit(solution)/shard_map/ppermute | solution.py:147
  27.1 2.2 %collective-permute-start.1 = (bf16[512,128]{1,0:T(8,128)(2,1)S(1)}, bf16[512,128]{1,0:T(8,128)(2,1)S(1)}, u32[]{:S(2)}, u32[]{:S(2)}) collective-permute-start(bf16[512,128]{1,0:T(8,128)(2,1)S(1)} %get-tuple-element.14), channel_id=1, source_target_pairs={{0,128},{128,256},{256,384},{384,0},{1,129},{129,257},{257,385},{3... | collective-permute-start | bytes 393224 | tf_op jit(solution)/shard_map/ppermute | solution.py:147
  29.3 4.3 %collective-permute-start.2 = (bf16[512,128]{1,0:T(8,128)(2,1)S(1)}, bf16[512,128]{1,0:T(8,128)(2,1)S(1)}, u32[]{:S(2)}, u32[]{:S(2)}) collective-permute-start(bf16[512,128]{1,0:T(8,128)(2,1)S(1)} %get-tuple-element.14), channel_id=1, source_target_pairs={{0,384},{128,0},{256,128},{384,256},{1,385},{129,1},{257,129},{385... | collective-permute-start | bytes 393224 | tf_op jit(solution)/shard_map/ppermute | solution.py:147
  33.6 4.8 %collective-permute-start.3 = (bf16[512,128]{1,0:T(8,128)(2,1)S(1)}, bf16[512,128]{1,0:T(8,128)(2,1)S(1)}, u32[]{:S(2)}, u32[]{:S(2)}) collective-permute-start(bf16[512,128]{1,0:T(8,128)(2,1)S(1)} %get-tuple-element.15), channel_id=1, source_target_pairs={{0,64},{32,96},{64,0},{96,32},{1,65},{33,97},{65,1},{97,33},{2,66}... | collective-permute-start | bytes 393224 | tf_op jit(solution)/shard_map/ppermute | solution.py:147
  38.4 2.3 %collective-permute-start.4 = (bf16[512,128]{1,0:T(8,128)(2,1)S(1)}, bf16[512,128]{1,0:T(8,128)(2,1)S(1)}, u32[]{:S(2)}, u32[]{:S(2)}) collective-permute-start(bf16[512,128]{1,0:T(8,128)(2,1)S(1)} %get-tuple-element.15), channel_id=1, source_target_pairs={{0,32},{32,64},{64,96},{96,0},{1,33},{33,65},{65,97},{97,1},{2,34}... | collective-permute-start | bytes 393224 | tf_op jit(solution)/shard_map/ppermute | solution.py:147
  40.7 4.2 %collective-permute-start.5 = (bf16[512,128]{1,0:T(8,128)(2,1)S(1)}, bf16[512,128]{1,0:T(8,128)(2,1)S(1)}, u32[]{:S(2)}, u32[]{:S(2)}) collective-permute-start(bf16[512,128]{1,0:T(8,128)(2,1)S(1)} %get-tuple-element.15), channel_id=1, source_target_pairs={{0,96},{32,0},{64,32},{96,64},{1,97},{33,1},{65,33},{97,65},{2,98}... | collective-permute-start | bytes 393224 | tf_op jit(solution)/shard_map/ppermute | solution.py:147
  44.9 0.7 collective-permute-done.4
  45.6 1.2 collective-permute-done.5
  46.9 1.9 collective-permute-start.10
  48.8 4.6 %collective-permute-start.11 = (bf16[4,512,128]{2,1,0:T(8,128)(2,1)S(1)}, bf16[4,512,128]{2,1,0:T(8,128)(2,1)}, u32[]{:S(2)}, u32[]{:S(2)}) collective-permute-start(bf16[4,512,128]{2,1,0:T(8,128)(2,1)S(1)} %pad_maximum_fusion.1.refs_4_), channel_id=1, source_target_pairs={{0,384},{128,0},{256,128},{384,256},{1,385},{129,1},{257,129},{385... | collective-permute-start | bytes 1572872 | tf_op jit(solution)/shard_map/ppermute | solution.py:147
  53.4 1.9 collective-permute-start.9
  55.4 3.8 %collective-permute-start.6 = (bf16[4,512,128]{2,1,0:T(8,128)(2,1)S(1)}, bf16[4,512,128]{2,1,0:T(8,128)(2,1)}, u32[]{:S(2)}, u32[]{:S(2)}) collective-permute-start(bf16[4,512,128]{2,1,0:T(8,128)(2,1)S(1)} %pad_maximum_fusion.refs_0_), channel_id=1, source_target_pairs={{0,64},{32,96},{64,0},{96,32},{1,65},{33,97},{65,1},{97,33},{2,66}... | collective-permute-start | bytes 1572872 | tf_op jit(solution)/shard_map/ppermute | solution.py:147
  59.2 4.0 %collective-permute-start.7 = (bf16[4,512,128]{2,1,0:T(8,128)(2,1)S(1)}, bf16[4,512,128]{2,1,0:T(8,128)(2,1)}, u32[]{:S(2)}, u32[]{:S(2)}) collective-permute-start(bf16[4,512,128]{2,1,0:T(8,128)(2,1)S(1)} %pad_maximum_fusion.refs_0_), channel_id=1, source_target_pairs={{0,32},{32,64},{64,96},{96,0},{1,33},{33,65},{65,97},{97,1},{2,34}... | collective-permute-start | bytes 1572872 | tf_op jit(solution)/shard_map/ppermute | solution.py:147
  63.2 0.8 copy-done.5
  64.0 4.3 %collective-permute-start.8 = (bf16[4,512,128]{2,1,0:T(8,128)(2,1)S(1)}, bf16[4,512,128]{2,1,0:T(8,128)(2,1)}, u32[]{:S(2)}, u32[]{:S(2)}) collective-permute-start(bf16[4,512,128]{2,1,0:T(8,128)(2,1)S(1)} %pad_maximum_fusion.refs_0_), channel_id=1, source_target_pairs={{0,96},{32,0},{64,32},{96,64},{1,97},{33,1},{65,33},{97,65},{2,98}... | collective-permute-start | bytes 1572872 | tf_op jit(solution)/shard_map/ppermute | solution.py:147
  68.4 2.0 %copy.7 = bf16[8,128,256]{1,2,0:T(8,128)(2,1)} copy(bf16[8,128,256]{2,1,0:T(8,128)(2,1)} %bitcast.23) | data formatting | bytes 1048576 | tf_op jit(solution)/shard_map/reshape | solution.py:331
  71.1 12.9 %collective-permute-done.7.refs_2_ = bf16[4,512,128]{2,1,0:T(8,128)(2,1)} collective-permute-done((bf16[4,512,128]{2,1,0:T(8,128)(2,1)S(1)}, bf16[4,512,128]{2,1,0:T(8,128)(2,1)}, u32[]{:S(2)}, u32[]{:S(2)}) %collective-permute-start.7) | collective-permute-done | bytes 524320 | tf_op jit(solution)/shard_map/ppermute | solution.py:147
  84.0 1.0 copy-done
  85.1 1.0 copy-done.6
  86.1 46.7 %shard_map.60.sk_ref = bf16[256,1024]{1,0:T(8,128)(2,1)S(1)} custom-call(bf16[4,512,128]{2,1,0:T(8,128)(2,1)S(1)} %pad_maximum_fusion.refs_0_, bf16[4,512,128]{2,1,0:T(8,128)(2,1)} %collective-permute-done.6.refs_1_, bf16[4,512,128]{2,1,0:T(8,128)(2,1)} %collective-permute-done.7.refs_2_, bf16[4,512,128]{2,1,0:T(8,128)(2,1)} %collective-permute-done.8.refs_3_, ...), custom_call_target="tpu_custom_call" | custom-call | tf_op jit(solution)/shard_map/pallas_call | solution.py:256
  132.8 0.8 copy-done.3
  133.6 1.0 copy-done.4
  134.7 13.5 %shard_map.61 = (bf16[256,1024]{1,0:T(8,128)(2,1)S(1)}, bf16[1024,256]{1,0:T(8,128)(2,1)}) custom-call(s32[1,1]{1,0:T(1,128)S(6)} %copy.10.rank_ref, bf16[1024,1024]{1,0:T(8,128)(2,1)S(1)} %bitcast.17, bf16[256,1024]{1,0:T(8,128)(2,1)S(1)} %copy-done.4), custom_call_target="tpu_custom_call" | custom-call | tf_op jit(solution)/shard_map/pallas_call | solution.py:305
  148.2 16.1 %all-to-all-start.1 = ((bf16[32,32,256]{2,1,0:T(8,128)(2,1)}), bf16[32,32,256]{2,1,0:T(8,128)(2,1)S(1)}, u32[]{:S(2)}, u32[]{:S(2)}) async-start(bf16[32,32,256]{2,1,0:T(8,128)(2,1)} %bitcast.11), calls=%async_computation.1 | async-start | bytes 1048576 | tf_op jit(solution)/shard_map/all_to_all | solution.py:334
  164.3 1.5 fusion
  165.8 32.0 %all-to-all-done.1 = bf16[32,32,256]{2,1,0:T(8,128)(2,1)S(1)} async-done(((bf16[32,32,256]{2,1,0:T(8,128)(2,1)}), bf16[32,32,256]{2,1,0:T(8,128)(2,1)S(1)}, u32[]{:S(2)}, u32[]{:S(2)}) %all-to-all-start.1) | async-done | bytes 524320 | tf_op jit(solution)/shard_map/all_to_all | solution.py:334
  197.9 0.8 copy.9
  (20 shorter events, 0.2 us)
Async XLA Ops:
  0.6 1.6 copy-start.1
  2.2 0.9 copy-start.7
  4.3 1.3 copy-start.2
  5.6 128.0 %all-to-all-start = ((bf16[32,32,1024]{2,1,0:T(8,128)(2,1)}), bf16[32,32,1024]{2,1,0:T(8,128)(2,1)S(1)}, u32[]{:S(2)}, u32[]{:S(2)}) async-start(bf16[32,32,1024]{2,1,0:T(8,128)(2,1)} %copy-done.2), calls=%async_computation | async-start | bytes 4194304 | tf_op jit(solution)/shard_map/all_to_all | solution.py:329
  22.4 18.3 %collective-permute-start = (bf16[512,128]{1,0:T(8,128)(2,1)S(1)}, bf16[512,128]{1,0:T(8,128)(2,1)S(1)}, u32[]{:S(2)}, u32[]{:S(2)}) collective-permute-start(bf16[512,128]{1,0:T(8,128)(2,1)S(1)} %get-tuple-element.14), channel_id=1, source_target_pairs={{0,256},{128,384},{256,0},{384,128},{1,257},{129,385},{257,1},{385... | collective-permute-start | bytes 393224 | tf_op jit(solution)/shard_map/ppermute | solution.py:147
  27.1 17.9 %collective-permute-start.1 = (bf16[512,128]{1,0:T(8,128)(2,1)S(1)}, bf16[512,128]{1,0:T(8,128)(2,1)S(1)}, u32[]{:S(2)}, u32[]{:S(2)}) collective-permute-start(bf16[512,128]{1,0:T(8,128)(2,1)S(1)} %get-tuple-element.14), channel_id=1, source_target_pairs={{0,128},{128,256},{256,384},{384,0},{1,129},{129,257},{257,385},{3... | collective-permute-start | bytes 393224 | tf_op jit(solution)/shard_map/ppermute | solution.py:147
  29.3 15.6 %collective-permute-start.2 = (bf16[512,128]{1,0:T(8,128)(2,1)S(1)}, bf16[512,128]{1,0:T(8,128)(2,1)S(1)}, u32[]{:S(2)}, u32[]{:S(2)}) collective-permute-start(bf16[512,128]{1,0:T(8,128)(2,1)S(1)} %get-tuple-element.14), channel_id=1, source_target_pairs={{0,384},{128,0},{256,128},{384,256},{1,385},{129,1},{257,129},{385... | collective-permute-start | bytes 393224 | tf_op jit(solution)/shard_map/ppermute | solution.py:147
  33.6 11.4 %collective-permute-start.3 = (bf16[512,128]{1,0:T(8,128)(2,1)S(1)}, bf16[512,128]{1,0:T(8,128)(2,1)S(1)}, u32[]{:S(2)}, u32[]{:S(2)}) collective-permute-start(bf16[512,128]{1,0:T(8,128)(2,1)S(1)} %get-tuple-element.15), channel_id=1, source_target_pairs={{0,64},{32,96},{64,0},{96,32},{1,65},{33,97},{65,1},{97,33},{2,66}... | collective-permute-start | bytes 393224 | tf_op jit(solution)/shard_map/ppermute | solution.py:147
  38.4 7.2 %collective-permute-start.4 = (bf16[512,128]{1,0:T(8,128)(2,1)S(1)}, bf16[512,128]{1,0:T(8,128)(2,1)S(1)}, u32[]{:S(2)}, u32[]{:S(2)}) collective-permute-start(bf16[512,128]{1,0:T(8,128)(2,1)S(1)} %get-tuple-element.15), channel_id=1, source_target_pairs={{0,32},{32,64},{64,96},{96,0},{1,33},{33,65},{65,97},{97,1},{2,34}... | collective-permute-start | bytes 393224 | tf_op jit(solution)/shard_map/ppermute | solution.py:147
  40.7 6.1 %collective-permute-start.5 = (bf16[512,128]{1,0:T(8,128)(2,1)S(1)}, bf16[512,128]{1,0:T(8,128)(2,1)S(1)}, u32[]{:S(2)}, u32[]{:S(2)}) collective-permute-start(bf16[512,128]{1,0:T(8,128)(2,1)S(1)} %get-tuple-element.15), channel_id=1, source_target_pairs={{0,96},{32,0},{64,32},{96,64},{1,97},{33,1},{65,33},{97,65},{2,98}... | collective-permute-start | bytes 393224 | tf_op jit(solution)/shard_map/ppermute | solution.py:147
  46.9 16.3 %collective-permute-start.10 = (bf16[4,512,128]{2,1,0:T(8,128)(2,1)S(1)}, bf16[4,512,128]{2,1,0:T(8,128)(2,1)S(1)}, u32[]{:S(2)}, u32[]{:S(2)}) collective-permute-start(bf16[4,512,128]{2,1,0:T(8,128)(2,1)S(1)} %pad_maximum_fusion.1.refs_4_), channel_id=1, source_target_pairs={{0,128},{128,256},{256,384},{384,0},{1,129},{129,257},{257,385},{3... | collective-permute-start | bytes 1572872 | tf_op jit(solution)/shard_map/ppermute | solution.py:147
  48.8 22.2 %collective-permute-start.11 = (bf16[4,512,128]{2,1,0:T(8,128)(2,1)S(1)}, bf16[4,512,128]{2,1,0:T(8,128)(2,1)}, u32[]{:S(2)}, u32[]{:S(2)}) collective-permute-start(bf16[4,512,128]{2,1,0:T(8,128)(2,1)S(1)} %pad_maximum_fusion.1.refs_4_), channel_id=1, source_target_pairs={{0,384},{128,0},{256,128},{384,256},{1,385},{129,1},{257,129},{385... | collective-permute-start | bytes 1572872 | tf_op jit(solution)/shard_map/ppermute | solution.py:147
  53.4 17.7 %collective-permute-start.9 = (bf16[4,512,128]{2,1,0:T(8,128)(2,1)S(1)}, bf16[4,512,128]{2,1,0:T(8,128)(2,1)}, u32[]{:S(2)}, u32[]{:S(2)}) collective-permute-start(bf16[4,512,128]{2,1,0:T(8,128)(2,1)S(1)} %pad_maximum_fusion.1.refs_4_), channel_id=1, source_target_pairs={{0,256},{128,384},{256,0},{384,128},{1,257},{129,385},{257,1},{385... | collective-permute-start | bytes 1572872 | tf_op jit(solution)/shard_map/ppermute | solution.py:147
  55.4 15.7 %collective-permute-start.6 = (bf16[4,512,128]{2,1,0:T(8,128)(2,1)S(1)}, bf16[4,512,128]{2,1,0:T(8,128)(2,1)}, u32[]{:S(2)}, u32[]{:S(2)}) collective-permute-start(bf16[4,512,128]{2,1,0:T(8,128)(2,1)S(1)} %pad_maximum_fusion.refs_0_), channel_id=1, source_target_pairs={{0,64},{32,96},{64,0},{96,32},{1,65},{33,97},{65,1},{97,33},{2,66}... | collective-permute-start | bytes 1572872 | tf_op jit(solution)/shard_map/ppermute | solution.py:147
  59.2 24.8 %collective-permute-start.7 = (bf16[4,512,128]{2,1,0:T(8,128)(2,1)S(1)}, bf16[4,512,128]{2,1,0:T(8,128)(2,1)}, u32[]{:S(2)}, u32[]{:S(2)}) collective-permute-start(bf16[4,512,128]{2,1,0:T(8,128)(2,1)S(1)} %pad_maximum_fusion.refs_0_), channel_id=1, source_target_pairs={{0,32},{32,64},{64,96},{96,0},{1,33},{33,65},{65,97},{97,1},{2,34}... | collective-permute-start | bytes 1572872 | tf_op jit(solution)/shard_map/ppermute | solution.py:147
  63.2 0.8 copy-start.5
  64.0 20.0 %collective-permute-start.8 = (bf16[4,512,128]{2,1,0:T(8,128)(2,1)S(1)}, bf16[4,512,128]{2,1,0:T(8,128)(2,1)}, u32[]{:S(2)}, u32[]{:S(2)}) collective-permute-start(bf16[4,512,128]{2,1,0:T(8,128)(2,1)S(1)} %pad_maximum_fusion.refs_0_), channel_id=1, source_target_pairs={{0,96},{32,0},{64,32},{96,64},{1,97},{33,1},{65,33},{97,65},{2,98}... | collective-permute-start | bytes 1572872 | tf_op jit(solution)/shard_map/ppermute | solution.py:147
  84.0 1.0 copy-start
  85.1 1.0 copy-start.6
  132.8 0.8 copy-start.3
  133.6 1.0 copy-start.4
  148.2 49.6 %all-to-all-start.1 = ((bf16[32,32,256]{2,1,0:T(8,128)(2,1)}), bf16[32,32,256]{2,1,0:T(8,128)(2,1)S(1)}, u32[]{:S(2)}, u32[]{:S(2)}) async-start(bf16[32,32,256]{2,1,0:T(8,128)(2,1)} %bitcast.11), calls=%async_computation.1 | async-start | bytes 1048576 | tf_op jit(solution)/shard_map/all_to_all | solution.py:334
where the time goes:
time: 200 us; the launch traced here: 199 us
  starting transfers between devices  75.9 us (38%)
  Pallas kernels  61.4 us (31%)
  waiting for transfers between devices  46.9 us (23%)
  local copies, waits for them, and re-layouts  11.4 us (6%)
    pallas_call x1, Pallas kernels, whiten(): pl.pallas_call(whiten_kernel, out_shape=jax.ShapeDtypeStruct((rmax, width...  46.7 us
    ppermute x12, starting transfers between devices, shifted(): lax.ppermute(value, axis, [(i, (i + shift) % side) for i in range(side)])  43 us
    all_to_all x1, waiting for transfers between devices, local(): lax.all_to_all(basis, 'tile', split_axis=0, concat_axis=1, tiled=True)  32 us
    all_to_all x1, starting transfers between devices, local(): lax.all_to_all(pieces, 'tile', split_axis=0, concat_axis=0, tiled=True)  16.7 us
    all_to_all x1, starting transfers between devices, local(): lax.all_to_all(basis, 'tile', split_axis=0, concat_axis=1, tiled=True)  16.1 us
    ppermute x12, waiting for transfers between devices, shifted(): lax.ppermute(value, axis, [(i, (i + shift) % side) for i in range(side)])  14.9 us
    pallas_call x1, Pallas kernels, basis_of(): pl.pallas_call(basis_kernel, out_shape=(jax.ShapeDtypeStruct((rmax, width...  13.5 us
    unnamed x16, local copies, waits for them, and re-layouts  8.56 us
  transfers between devices with their start and end apart: 14, of which 5 were waited for; matrix products, arithmetic and copies ran while one was open for 2% of the time, Pallas kernels for 24%

commit v1 on v0

--- a/solution.py
+++ b/solution.py
@@ -11,6 +11,8 @@
 DAMPING = 0.1
 NB = 128
 STRIP = 8
+PREPARE_STEPS = 4
+GRANT = 56 * 1024 * 1024
 F32 = jnp.float32
 BF16 = jnp.bfloat16
 
@@ -113,17 +115,26 @@
         inv_ref[s * STRIP : (s + 1) * STRIP, :] = rows
 
 
-def prepare_kernel(x_ref, w_ref, high_ref, low_ref, pieces_ref, sems):
-    pieces, _, width = pieces_ref.shape
-    copies = [
-        pltpu.make_async_copy(w_ref.at[:, pl.ds(t * width, width)], pieces_ref.at[t], sems.at[t]) for t in range(pieces)
+def prepare_kernel(x_ref, w_ref, high_ref, low_ref, pieces_ref, hold_ref, in_sems, out_sems):
+    pieces, _, width = hold_ref.shape
+    group = pieces // PREPARE_STEPS
+    inward = [
+        pltpu.make_async_copy(w_ref.at[:, pl.ds(t * width, width)], hold_ref.at[t], in_sems.at[t]) for t in range(pieces)
     ]
-    for copy in copies:
+    outward = [
+        pltpu.make_async_copy(hold_ref.at[pl.ds(g * group, group)], pieces_ref.at[pl.ds(g * group, group)], out_sems.at[g])
+        for g in range(PREPARE_STEPS)
+    ]
+    for copy in inward:
         copy.start()
     half = high_ref.shape[0]
     high_ref[...] = x_ref[:, :half].T
     low_ref[...] = x_ref[:, half:].T
-    for copy in copies:
+    for g in range(PREPARE_STEPS):
+        for copy in inward[g * group : (g + 1) * group]:
+            copy.wait()
+        outward[g].start()
+    for copy in outward:
         copy.wait()
 
 
@@ -135,10 +146,18 @@
     return pl.pallas_call(
         prepare_kernel,
         out_shape=(half, half, jax.ShapeDtypeStruct((pieces, rows, width), weights.dtype)),
-        in_specs=[pl.BlockSpec(memory_space=pltpu.VMEM), pl.BlockSpec(memory_space=pltpu.HBM)],
-        out_specs=(pl.BlockSpec(memory_space=pltpu.VMEM),) * 3,
-        scratch_shapes=[pltpu.SemaphoreType.DMA((pieces,))],
-        compiler_params=pltpu.CompilerParams(vmem_limit_bytes=16 * 1024 * 1024),
+        in_specs=[pl.BlockSpec(memory_space=pltpu.VMEM), pl.BlockSpec(memory_space=pl.ANY)],
+        out_specs=(
+            pl.BlockSpec(memory_space=pltpu.VMEM),
+            pl.BlockSpec(memory_space=pltpu.VMEM),
+            pl.BlockSpec(memory_space=pl.ANY),
+        ),
+        scratch_shapes=[
+            pltpu.VMEM((pieces, rows, width), weights.dtype),
+            pltpu.SemaphoreType.DMA((pieces,)),
+            pltpu.SemaphoreType.DMA((PREPARE_STEPS,)),
+        ],
+        compiler_params=pltpu.CompilerParams(vmem_limit_bytes=GRANT),
     )(x, weights)
 
 
@@ -154,7 +173,11 @@
     lines = [tuple(shifted(half, axis, d) for d in FAR_FIRST) for half, axis in ((high, "x"), (low, "y"))]
     lines = lax.optimization_barrier(lines)
     lines = [jnp.stack((half,) + line) for half, line in zip((high, low), lines)]
-    return [(line,) + tuple(shifted(line, axis, d) for d in FAR_FIRST) for line, axis in zip(lines, ("y", "x"))]
+    ahead = [shifted(line, axis, -1) for line, axis in zip(lines, ("y", "x"))]
+    back = [shifted(line, axis, 1) for line, axis in zip(lines, ("y", "x"))]
+    ahead = lax.optimization_barrier(ahead)
+    far = [shifted(line, axis, -1) for line, axis in zip(ahead, ("y", "x"))]
+    return list(zip(lines, far, back, ahead))
 
 
 def whiten_kernel(*refs):

time: 200 us -> 193 us (0.965)
  local copies, waits for them, and re-layouts: 11.4 us -> 5.75 us
  waiting for transfers between devices: 46.9 us -> 42.6 us
  Pallas kernels: 61.4 us -> 64.8 us
    unnamed x16 -> x10, local copies, waits for them, and re-layouts: 8.56 us -> 2.88 us
    ppermute x12, waiting for transfers between devices: 14.9 us -> 10.6 us  [shifted(): lax.ppermute(value, axis, [(i, (i + shift) % side) for i in range(side)])]
    pallas_call x1, Pallas kernels: 1.12 us -> 4.37 us  [prepare(): pl.pallas_call(prepare_kernel, out_shape=(half, half, jax.ShapeDtypeStruc...]
  transfers between devices with their start and end apart: 14 -> 14, of which waited for: 5 -> 7; matrix products, arithmetic and copies ran while one was open for 2% -> 2% of each run, Pallas kernels for 24% -> 24%
where the time goes in v1:
time: 193 us; the launch traced here: 192 us
  starting transfers between devices  75.3 us (39%)
  Pallas kernels  64.8 us (34%)
  waiting for transfers between devices  42.6 us (22%)
  local copies, waits for them, and re-layouts  5.75 us (3%)
    pallas_call x1, Pallas kernels, whiten(): pl.pallas_call(whiten_kernel, out_shape=jax.ShapeDtypeStruct((rmax, width...  46.9 us
    ppermute x12, starting transfers between devices, shifted(): lax.ppermute(value, axis, [(i, (i + shift) % side) for i in range(side)])  42.3 us
    all_to_all x1, waiting for transfers between devices, local(): lax.all_to_all(basis, 'tile', split_axis=0, concat_axis=1, tiled=True)  32 us
    all_to_all x1, starting transfers between devices, local(): lax.all_to_all(pieces, 'tile', split_axis=0, concat_axis=0, tiled=True)  16.9 us
    all_to_all x1, starting transfers between devices, local(): lax.all_to_all(basis, 'tile', split_axis=0, concat_axis=1, tiled=True)  16.1 us
    pallas_call x1, Pallas kernels, basis_of(): pl.pallas_call(basis_kernel, out_shape=(jax.ShapeDtypeStruct((rmax, width...  13.5 us
    ppermute x12, waiting for transfers between devices, shifted(): lax.ppermute(value, axis, [(i, (i + shift) % side) for i in range(side)])  10.6 us
    pallas_call x1, Pallas kernels, prepare(): pl.pallas_call(prepare_kernel, out_shape=(half, half, jax.ShapeDtypeStruc...  4.37 us
  transfers between devices with their start and end apart: 14, of which 7 were waited for; matrix products, arithmetic and copies ran while one was open for 2% of the time, Pallas kernels for 24%

profile of v1, /device:TPU:1, one launch (start us, length us, event | category | flops | bytes accessed | tf_op | source)
XLA Modules:
  0.0 191.6 jit_solution(17294233734278857564)
XLA Ops:
  0.6 4.4 %shard_map.59 = (bf16[512,128]{1,0:T(8,128)(2,1)}, bf16[512,128]{1,0:T(8,128)(2,1)}, bf16[32,32,1024]{2,1,0:T(8,128)(2,1)}) custom-call(bf16[128,1024]{1,0:T(8,128)(2,1)} %x_ref.1, bf16[32,32768]{1,0:T(8,128)(2,1)} %w_ref.1), custom_call_target="tpu_custom_call" | custom-call | tf_op jit(solution)/shard_map/pallas_call | solution.py:146
  5.0 16.9 %all-to-all-start = ((bf16[32,32,1024]{2,1,0:T(8,128)(2,1)}), bf16[32,32,1024]{2,1,0:T(8,128)(2,1)S(1)}, u32[]{:S(2)}, u32[]{:S(2)}) async-start(bf16[32,32,1024]{2,1,0:T(8,128)(2,1)} %get-tuple-element.15), calls=%async_computation | async-start | bytes 4194304 | tf_op jit(solution)/shard_map/all_to_all | solution.py:352
  21.9 4.7 %collective-permute-start = (bf16[512,128]{1,0:T(8,128)(2,1)S(1)}, bf16[512,128]{1,0:T(8,128)(2,1)S(1)}, u32[]{:S(2)}, u32[]{:S(2)}) collective-permute-start(bf16[512,128]{1,0:T(8,128)(2,1)S(1)} %copy-done.3), channel_id=1, source_target_pairs={{0,256},{128,384},{256,0},{384,128},{1,257},{129,385},{257,1},{385... | collective-permute-start | bytes 393224 | tf_op jit(solution)/shard_map/ppermute | solution.py:166
  26.6 2.2 %collective-permute-start.1 = (bf16[512,128]{1,0:T(8,128)(2,1)S(1)}, bf16[512,128]{1,0:T(8,128)(2,1)S(1)}, u32[]{:S(2)}, u32[]{:S(2)}) collective-permute-start(bf16[512,128]{1,0:T(8,128)(2,1)S(1)} %copy-done.3), channel_id=1, source_target_pairs={{0,128},{128,256},{256,384},{384,0},{1,129},{129,257},{257,385},{3... | collective-permute-start | bytes 393224 | tf_op jit(solution)/shard_map/ppermute | solution.py:166
  28.8 4.3 %collective-permute-start.2 = (bf16[512,128]{1,0:T(8,128)(2,1)S(1)}, bf16[512,128]{1,0:T(8,128)(2,1)S(1)}, u32[]{:S(2)}, u32[]{:S(2)}) collective-permute-start(bf16[512,128]{1,0:T(8,128)(2,1)S(1)} %copy-done.3), channel_id=1, source_target_pairs={{0,384},{128,0},{256,128},{384,256},{1,385},{129,1},{257,129},{385... | collective-permute-start | bytes 393224 | tf_op jit(solution)/shard_map/ppermute | solution.py:166
  33.1 4.8 %collective-permute-start.3 = (bf16[512,128]{1,0:T(8,128)(2,1)S(1)}, bf16[512,128]{1,0:T(8,128)(2,1)S(1)}, u32[]{:S(2)}, u32[]{:S(2)}) collective-permute-start(bf16[512,128]{1,0:T(8,128)(2,1)S(1)} %copy-done.4), channel_id=1, source_target_pairs={{0,64},{32,96},{64,0},{96,32},{1,65},{33,97},{65,1},{97,33},{2,66}... | collective-permute-start | bytes 393224 | tf_op jit(solution)/shard_map/ppermute | solution.py:166
  37.9 2.3 %collective-permute-start.4 = (bf16[512,128]{1,0:T(8,128)(2,1)S(1)}, bf16[512,128]{1,0:T(8,128)(2,1)S(1)}, u32[]{:S(2)}, u32[]{:S(2)}) collective-permute-start(bf16[512,128]{1,0:T(8,128)(2,1)S(1)} %copy-done.4), channel_id=1, source_target_pairs={{0,32},{32,64},{64,96},{96,0},{1,33},{33,65},{65,97},{97,1},{2,34}... | collective-permute-start | bytes 393224 | tf_op jit(solution)/shard_map/ppermute | solution.py:166
  40.3 4.2 %collective-permute-start.5 = (bf16[512,128]{1,0:T(8,128)(2,1)S(1)}, bf16[512,128]{1,0:T(8,128)(2,1)S(1)}, u32[]{:S(2)}, u32[]{:S(2)}) collective-permute-start(bf16[512,128]{1,0:T(8,128)(2,1)S(1)} %copy-done.4), channel_id=1, source_target_pairs={{0,96},{32,0},{64,32},{96,64},{1,97},{33,1},{65,33},{97,65},{2,98}... | collective-permute-start | bytes 393224 | tf_op jit(solution)/shard_map/ppermute | solution.py:166
  44.5 0.7 collective-permute-done.4
  45.2 1.2 collective-permute-done.5
  46.4 0.1 pad_maximum_fusion.1.refs_4_
  46.5 1.9 %collective-permute-start.7 = (bf16[4,512,128]{2,1,0:T(8,128)(2,1)S(1)}, bf16[4,512,128]{2,1,0:T(8,128)(2,1)}, u32[]{:S(2)}, u32[]{:S(2)}) collective-permute-start(bf16[4,512,128]{2,1,0:T(8,128)(2,1)S(1)} %pad_maximum_fusion.1.refs_4_), channel_id=1, source_target_pairs={{0,384},{128,0},{256,128},{384,256},{1,385},{129,1},{257,129},{385... | collective-permute-start | bytes 1572872 | tf_op jit(solution)/shard_map/ppermute | solution.py:166
  48.4 0.1 pad_maximum_fusion.refs_0_
  48.5 5.3 %collective-permute-start.6 = (bf16[4,512,128]{2,1,0:T(8,128)(2,1)S(1)}, bf16[4,512,128]{2,1,0:T(8,128)(2,1)}, u32[]{:S(2)}, u32[]{:S(2)}) collective-permute-start(bf16[4,512,128]{2,1,0:T(8,128)(2,1)S(1)} %pad_maximum_fusion.refs_0_), channel_id=1, source_target_pairs={{0,96},{32,0},{64,32},{96,64},{1,97},{33,1},{65,33},{97,65},{2,98}... | collective-permute-start | bytes 1572872 | tf_op jit(solution)/shard_map/ppermute | solution.py:166
  53.8 3.4 %collective-permute-start.11 = (bf16[4,512,128]{2,1,0:T(8,128)(2,1)S(1)}, bf16[4,512,128]{2,1,0:T(8,128)(2,1)}, u32[]{:S(2)}, u32[]{:S(2)}) collective-permute-start(bf16[4,512,128]{2,1,0:T(8,128)(2,1)S(1)} %pad_maximum_fusion.1.refs_4_), channel_id=1, source_target_pairs={{0,128},{128,256},{256,384},{384,0},{1,129},{129,257},{257,385},{3... | collective-permute-start | bytes 1572872 | tf_op jit(solution)/shard_map/ppermute | solution.py:166
  57.1 1.9 %collective-permute-start.9 = (bf16[4,512,128]{2,1,0:T(8,128)(2,1)S(1)}, bf16[4,512,128]{2,1,0:T(8,128)(2,1)}, u32[]{:S(2)}, u32[]{:S(2)}) collective-permute-start(bf16[4,512,128]{2,1,0:T(8,128)(2,1)S(1)} %pad_maximum_fusion.refs_0_), channel_id=1, source_target_pairs={{0,32},{32,64},{64,96},{96,0},{1,33},{33,65},{65,97},{97,1},{2,34}... | collective-permute-start | bytes 1572872 | tf_op jit(solution)/shard_map/ppermute | solution.py:166
  59.1 0.3 collective-permute-done.7.refs_7_
  59.4 3.1 %collective-permute-done.6.refs_3_ = bf16[4,512,128]{2,1,0:T(8,128)(2,1)} collective-permute-done((bf16[4,512,128]{2,1,0:T(8,128)(2,1)S(1)}, bf16[4,512,128]{2,1,0:T(8,128)(2,1)}, u32[]{:S(2)}, u32[]{:S(2)}) %collective-permute-start.6) | collective-permute-done | bytes 524320 | tf_op jit(solution)/shard_map/ppermute | solution.py:166
  62.5 1.9 collective-permute-start.10
  64.4 5.4 %collective-permute-start.8 = (bf16[4,512,128]{2,1,0:T(8,128)(2,1)}, bf16[4,512,128]{2,1,0:T(8,128)(2,1)}, u32[]{:S(2)}, u32[]{:S(2)}) collective-permute-start(bf16[4,512,128]{2,1,0:T(8,128)(2,1)} %collective-permute-done.6.refs_3_), channel_id=1, source_target_pairs={{0,96},{32,0},{64,32},{96,64},{1,97},{33,1},{65,33},{97,65},{2,98}... | collective-permute-start | bytes 1572872 | tf_op jit(solution)/shard_map/ppermute | solution.py:166
  69.8 2.0 %copy.7 = bf16[8,128,256]{1,2,0:T(8,128)(2,1)} copy(bf16[8,128,256]{2,1,0:T(8,128)(2,1)} %bitcast.21) | data formatting | bytes 1048576 | tf_op jit(solution)/shard_map/reshape | solution.py:354
  72.5 2.1 %collective-permute-done.10.refs_5_ = bf16[4,512,128]{2,1,0:T(8,128)(2,1)} collective-permute-done((bf16[4,512,128]{2,1,0:T(8,128)(2,1)}, bf16[4,512,128]{2,1,0:T(8,128)(2,1)}, u32[]{:S(2)}, u32[]{:S(2)}) %collective-permute-start.10) | collective-permute-done | bytes 524320 | tf_op jit(solution)/shard_map/ppermute | solution.py:166
  74.7 3.1 %collective-permute-done.8.refs_1_ = bf16[4,512,128]{2,1,0:T(8,128)(2,1)} collective-permute-done((bf16[4,512,128]{2,1,0:T(8,128)(2,1)}, bf16[4,512,128]{2,1,0:T(8,128)(2,1)}, u32[]{:S(2)}, u32[]{:S(2)}) %collective-permute-start.8) | collective-permute-done | bytes 524320 | tf_op jit(solution)/shard_map/ppermute | solution.py:166
  77.8 1.0 copy-done
  78.8 46.9 %shard_map.60.sk_ref = bf16[256,1024]{1,0:T(8,128)(2,1)S(1)} custom-call(bf16[4,512,128]{2,1,0:T(8,128)(2,1)S(1)} %pad_maximum_fusion.refs_0_, bf16[4,512,128]{2,1,0:T(8,128)(2,1)} %collective-permute-done.8.refs_1_, bf16[4,512,128]{2,1,0:T(8,128)(2,1)} %collective-permute-done.9.refs_2_, bf16[4,512,128]{2,1,0:T(8,128)(2,1)} %collective-permute-done.6.refs_3_, ...), custom_call_target="tpu_custom_call" | custom-call | tf_op jit(solution)/shard_map/pallas_call | solution.py:279
  125.7 0.8 copy-done.1
  126.5 1.0 copy-done.2
  127.6 13.5 %shard_map.61 = (bf16[256,1024]{1,0:T(8,128)(2,1)S(1)}, bf16[1024,256]{1,0:T(8,128)(2,1)}) custom-call(s32[1,1]{1,0:T(1,128)S(6)} %copy.10.rank_ref, bf16[1024,1024]{1,0:T(8,128)(2,1)S(1)} %bitcast.17, bf16[256,1024]{1,0:T(8,128)(2,1)S(1)} %copy-done.2), custom_call_target="tpu_custom_call" | custom-call | tf_op jit(solution)/shard_map/pallas_call | solution.py:328
  141.1 16.1 %all-to-all-start.1 = ((bf16[32,32,256]{2,1,0:T(8,128)(2,1)}), bf16[32,32,256]{2,1,0:T(8,128)(2,1)S(1)}, u32[]{:S(2)}, u32[]{:S(2)}) async-start(bf16[32,32,256]{2,1,0:T(8,128)(2,1)} %bitcast.11), calls=%async_computation.1 | async-start | bytes 1048576 | tf_op jit(solution)/shard_map/all_to_all | solution.py:357
  157.2 1.5 fusion
  158.8 32.0 %all-to-all-done.1 = bf16[32,32,256]{2,1,0:T(8,128)(2,1)S(1)} async-done(((bf16[32,32,256]{2,1,0:T(8,128)(2,1)}), bf16[32,32,256]{2,1,0:T(8,128)(2,1)S(1)}, u32[]{:S(2)}, u32[]{:S(2)}) %all-to-all-start.1) | async-done | bytes 524320 | tf_op jit(solution)/shard_map/all_to_all | solution.py:357
  190.8 0.8 copy.9
  (14 shorter events, 0.0 us)
Async XLA Ops:
  5.0 16.9 %copy-start.3 = (bf16[512,128]{1,0:T(8,128)(2,1)S(1)}, bf16[512,128]{1,0:T(8,128)(2,1)}, u32[]{:S(2)}) copy-start(bf16[512,128]{1,0:T(8,128)(2,1)} %get-tuple-element.16) | copy-start | bytes 393220
  5.0 28.1 %copy-start.4 = (bf16[512,128]{1,0:T(8,128)(2,1)S(1)}, bf16[512,128]{1,0:T(8,128)(2,1)}, u32[]{:S(2)}) copy-start(bf16[512,128]{1,0:T(8,128)(2,1)} %get-tuple-element.17) | copy-start | bytes 393220
  5.0 121.5 %all-to-all-start = ((bf16[32,32,1024]{2,1,0:T(8,128)(2,1)}), bf16[32,32,1024]{2,1,0:T(8,128)(2,1)S(1)}, u32[]{:S(2)}, u32[]{:S(2)}) async-start(bf16[32,32,1024]{2,1,0:T(8,128)(2,1)} %get-tuple-element.15), calls=%async_computation | async-start | bytes 4194304 | tf_op jit(solution)/shard_map/all_to_all | solution.py:352
  21.9 18.3 %collective-permute-start = (bf16[512,128]{1,0:T(8,128)(2,1)S(1)}, bf16[512,128]{1,0:T(8,128)(2,1)S(1)}, u32[]{:S(2)}, u32[]{:S(2)}) collective-permute-start(bf16[512,128]{1,0:T(8,128)(2,1)S(1)} %copy-done.3), channel_id=1, source_target_pairs={{0,256},{128,384},{256,0},{384,128},{1,257},{129,385},{257,1},{385... | collective-permute-start | bytes 393224 | tf_op jit(solution)/shard_map/ppermute | solution.py:166
  26.6 17.9 %collective-permute-start.1 = (bf16[512,128]{1,0:T(8,128)(2,1)S(1)}, bf16[512,128]{1,0:T(8,128)(2,1)S(1)}, u32[]{:S(2)}, u32[]{:S(2)}) collective-permute-start(bf16[512,128]{1,0:T(8,128)(2,1)S(1)} %copy-done.3), channel_id=1, source_target_pairs={{0,128},{128,256},{256,384},{384,0},{1,129},{129,257},{257,385},{3... | collective-permute-start | bytes 393224 | tf_op jit(solution)/shard_map/ppermute | solution.py:166
  28.8 15.7 %collective-permute-start.2 = (bf16[512,128]{1,0:T(8,128)(2,1)S(1)}, bf16[512,128]{1,0:T(8,128)(2,1)S(1)}, u32[]{:S(2)}, u32[]{:S(2)}) collective-permute-start(bf16[512,128]{1,0:T(8,128)(2,1)S(1)} %copy-done.3), channel_id=1, source_target_pairs={{0,384},{128,0},{256,128},{384,256},{1,385},{129,1},{257,129},{385... | collective-permute-start | bytes 393224 | tf_op jit(solution)/shard_map/ppermute | solution.py:166
  33.1 11.4 %collective-permute-start.3 = (bf16[512,128]{1,0:T(8,128)(2,1)S(1)}, bf16[512,128]{1,0:T(8,128)(2,1)S(1)}, u32[]{:S(2)}, u32[]{:S(2)}) collective-permute-start(bf16[512,128]{1,0:T(8,128)(2,1)S(1)} %copy-done.4), channel_id=1, source_target_pairs={{0,64},{32,96},{64,0},{96,32},{1,65},{33,97},{65,1},{97,33},{2,66}... | collective-permute-start | bytes 393224 | tf_op jit(solution)/shard_map/ppermute | solution.py:166
  37.9 7.2 %collective-permute-start.4 = (bf16[512,128]{1,0:T(8,128)(2,1)S(1)}, bf16[512,128]{1,0:T(8,128)(2,1)S(1)}, u32[]{:S(2)}, u32[]{:S(2)}) collective-permute-start(bf16[512,128]{1,0:T(8,128)(2,1)S(1)} %copy-done.4), channel_id=1, source_target_pairs={{0,32},{32,64},{64,96},{96,0},{1,33},{33,65},{65,97},{97,1},{2,34}... | collective-permute-start | bytes 393224 | tf_op jit(solution)/shard_map/ppermute | solution.py:166
  40.3 6.1 %collective-permute-start.5 = (bf16[512,128]{1,0:T(8,128)(2,1)S(1)}, bf16[512,128]{1,0:T(8,128)(2,1)S(1)}, u32[]{:S(2)}, u32[]{:S(2)}) collective-permute-start(bf16[512,128]{1,0:T(8,128)(2,1)S(1)} %copy-done.4), channel_id=1, source_target_pairs={{0,96},{32,0},{64,32},{96,64},{1,97},{33,1},{65,33},{97,65},{2,98}... | collective-permute-start | bytes 393224 | tf_op jit(solution)/shard_map/ppermute | solution.py:166
  46.5 12.9 %collective-permute-start.7 = (bf16[4,512,128]{2,1,0:T(8,128)(2,1)S(1)}, bf16[4,512,128]{2,1,0:T(8,128)(2,1)}, u32[]{:S(2)}, u32[]{:S(2)}) collective-permute-start(bf16[4,512,128]{2,1,0:T(8,128)(2,1)S(1)} %pad_maximum_fusion.1.refs_4_), channel_id=1, source_target_pairs={{0,384},{128,0},{256,128},{384,256},{1,385},{129,1},{257,129},{385... | collective-permute-start | bytes 1572872 | tf_op jit(solution)/shard_map/ppermute | solution.py:166
  48.5 14.0 %collective-permute-start.6 = (bf16[4,512,128]{2,1,0:T(8,128)(2,1)S(1)}, bf16[4,512,128]{2,1,0:T(8,128)(2,1)}, u32[]{:S(2)}, u32[]{:S(2)}) collective-permute-start(bf16[4,512,128]{2,1,0:T(8,128)(2,1)S(1)} %pad_maximum_fusion.refs_0_), channel_id=1, source_target_pairs={{0,96},{32,0},{64,32},{96,64},{1,97},{33,1},{65,33},{97,65},{2,98}... | collective-permute-start | bytes 1572872 | tf_op jit(solution)/shard_map/ppermute | solution.py:166
  53.8 18.8 %collective-permute-start.11 = (bf16[4,512,128]{2,1,0:T(8,128)(2,1)S(1)}, bf16[4,512,128]{2,1,0:T(8,128)(2,1)}, u32[]{:S(2)}, u32[]{:S(2)}) collective-permute-start(bf16[4,512,128]{2,1,0:T(8,128)(2,1)S(1)} %pad_maximum_fusion.1.refs_4_), channel_id=1, source_target_pairs={{0,128},{128,256},{256,384},{384,0},{1,129},{129,257},{257,385},{3... | collective-permute-start | bytes 1572872 | tf_op jit(solution)/shard_map/ppermute | solution.py:166
  57.1 15.4 %collective-permute-start.9 = (bf16[4,512,128]{2,1,0:T(8,128)(2,1)S(1)}, bf16[4,512,128]{2,1,0:T(8,128)(2,1)}, u32[]{:S(2)}, u32[]{:S(2)}) collective-permute-start(bf16[4,512,128]{2,1,0:T(8,128)(2,1)S(1)} %pad_maximum_fusion.refs_0_), channel_id=1, source_target_pairs={{0,32},{32,64},{64,96},{96,0},{1,33},{33,65},{65,97},{97,1},{2,34}... | collective-permute-start | bytes 1572872 | tf_op jit(solution)/shard_map/ppermute | solution.py:166
  62.5 12.2 %collective-permute-start.10 = (bf16[4,512,128]{2,1,0:T(8,128)(2,1)}, bf16[4,512,128]{2,1,0:T(8,128)(2,1)}, u32[]{:S(2)}, u32[]{:S(2)}) collective-permute-start(bf16[4,512,128]{2,1,0:T(8,128)(2,1)} %collective-permute-done.7.refs_7_), channel_id=1, source_target_pairs={{0,384},{128,0},{256,128},{384,256},{1,385},{129,1},{257,129},{385... | collective-permute-start | bytes 1572872 | tf_op jit(solution)/shard_map/ppermute | solution.py:166
  64.4 13.4 %collective-permute-start.8 = (bf16[4,512,128]{2,1,0:T(8,128)(2,1)}, bf16[4,512,128]{2,1,0:T(8,128)(2,1)}, u32[]{:S(2)}, u32[]{:S(2)}) collective-permute-start(bf16[4,512,128]{2,1,0:T(8,128)(2,1)} %collective-permute-done.6.refs_3_), channel_id=1, source_target_pairs={{0,96},{32,0},{64,32},{96,64},{1,97},{33,1},{65,33},{97,65},{2,98}... | collective-permute-start | bytes 1572872 | tf_op jit(solution)/shard_map/ppermute | solution.py:166
  77.8 1.0 copy-start
  125.7 0.8 copy-start.1
  126.5 1.0 copy-start.2
  141.1 49.7 %all-to-all-start.1 = ((bf16[32,32,256]{2,1,0:T(8,128)(2,1)}), bf16[32,32,256]{2,1,0:T(8,128)(2,1)S(1)}, u32[]{:S(2)}, u32[]{:S(2)}) async-start(bf16[32,32,256]{2,1,0:T(8,128)(2,1)} %bitcast.11), calls=%async_computation.1 | async-start | bytes 1048576 | tf_op jit(solution)/shard_map/all_to_all | solution.py:357

commit v2 on v1

--- a/solution.py
+++ b/solution.py
@@ -193,7 +193,11 @@
         parts = [first[y][x + d] if upper else second[x + d][y] for d in range(2)]
         return jnp.concatenate(parts, axis=1)
 
-    for c in range(panels // 2):
+    lane = lax.broadcasted_iota(jnp.int32, (NB, NB), 1)
+    sub = lax.broadcasted_iota(jnp.int32, (NB, NB), 0)
+    diag = lane == sub
+
+    def gram_columns(c):
         lo = c * wide
         top = bottom = None
         for x in range(0, inner, 2):
@@ -216,20 +220,41 @@
         a_ref[2 * c, from_row:, :] = bottom[:, :NB]
         a_ref[2 * c + 1, from_row:, :] = bottom[:, NB:]
 
-    lane = lax.broadcasted_iota(jnp.int32, (NB, NB), 1)
-    sub = lax.broadcasted_iota(jnp.int32, (NB, NB), 0)
-    diag = lane == sub
-    trace = jnp.zeros((NB, NB), F32)
-    for c in range(panels):
-        trace = trace + jnp.where(diag, a_ref[c, c * NB : (c + 1) * NB, :], 0.0)
-    damp = jnp.sum(trace) * (DAMPING / width)
-    for c in range(panels):
+    def square_sum():
+        total = jnp.zeros((STRIP, NB), F32)
+        for parts in (first, second):
+            for part in parts:
+                for d in range(inner):
+                    values = part[d].astype(F32)
+                    total = total + jnp.sum((values * values).reshape(half // STRIP, STRIP, NB), axis=0)
+        return jnp.sum(total)
+
+    damp = square_sum() * (DAMPING / width)
+
+    def damped(c):
         block = a_ref[c, c * NB : (c + 1) * NB, :]
-        a_ref[c, c * NB : (c + 1) * NB, :] = jnp.where(diag, block + damp, block)
-
-    inv_ref[...] = jnp.zeros_like(inv_ref)
+        block = jnp.where(diag, block + damp, block)
+        a_ref[c, c * NB : (c + 1) * NB, :] = block
+        return block
+
+    def strips_of(block):
+        return [block[s * STRIP : (s + 1) * STRIP, :] for s in range(NB // STRIP)]
+
+    gram_columns(0)
+    block = damped(0)
+    for c in range(1, panels // 2):
+        gram_columns(c)
+    for c in range(1, panels):
+        damped(c)
     acc_ref[...] = jnp.zeros_like(acc_ref)
-    d_ref[...] = a_ref[0, :NB, :]
+    factor_into(strips_of(block), inv_ref)
+
+    def near_block(p, nxt):
+        rows_n = pl.ds(pl.multiple_of(nxt * NB, NB), NB)
+        near = dot3(a_ref[p, rows_n, :], inv_ref[...], NT)
+        d_ref[...] = a_ref[nxt, rows_n, :] - dot3(near, near, NT)
+
+    near_block(0, 1)
 
     tall_row = lax.broadcasted_iota(jnp.int32, (width, NB), 0)
     tall_lane = lax.broadcasted_iota(jnp.int32, (width, NB), 1)
@@ -240,13 +265,13 @@
         panel = dot(jnp.concatenate([ph, pm], axis=1), jnp.concatenate([ih, ih], axis=1), NT) + dot(ph, il, NT)
         return jnp.where(tall_row >= tall_lane + p * NB, panel, 0.0)
 
-    def sketch_in(p, both):
-        part = sketch_ref[p]
-        acc_ref[...] += dot(jnp.concatenate([part, part], axis=1), both, NT)
+    def sketch_of(p):
+        part = sketch_ref[pl.ds(pl.multiple_of(p * NB, NB), NB), :].T
+        return jnp.concatenate([part, part], axis=1)
 
     def step(p, carry):
-        strips = [d_ref[s * STRIP : (s + 1) * STRIP, :] for s in range(NB // STRIP)]
-        before = jnp.maximum(p - 1, 0)
+        strips = strips_of(d_ref[...])
+        before = p - 1
         panel = panel_of(before, inv_ref[...])
         hi, lo16 = split2(panel)
         both = jnp.concatenate([hi, lo16], axis=1)
@@ -259,23 +284,23 @@
             off = dot(both[lo:], twice[lo : lo + wide], NT) + dot(hi[lo:], lo_r[lo : lo + wide], NT)
             a_ref[2 * c, lo:, :] -= off[:, :NB]
             a_ref[2 * c + 1, lo:, :] -= off[:, NB:]
-        sketch_in(before, both)
+        acc_ref[...] += dot(sketch_of(before), both, NT)
         factor_into(strips, inv_ref)
-        nxt = jnp.minimum(p + 1, panels - 1)
-        rows_n = pl.ds(pl.multiple_of(nxt * NB, NB), NB)
-        near = dot3(a_ref[p, rows_n, :], inv_ref[...], NT)
-        d_ref[...] = a_ref[nxt, rows_n, :] - dot3(near, near, NT)
+        near_block(p, jnp.minimum(p + 1, panels - 1))
         return carry
 
-    lax.fori_loop(0, panels, step, 0)
-    hi, lo16 = split2(panel_of(panels - 1, inv_ref[...]))
-    sketch_in(panels - 1, jnp.concatenate([hi, lo16], axis=1))
-    out_ref[...] = acc_ref[...].astype(BF16)
-
-
-def whiten(first, second, sketch_t):
+    lax.fori_loop(1, panels, step, 0)
+    top = width - NB
+    corner = dot3(a_ref[panels - 1, top:, :], inv_ref[...], NT)
+    hi, lo16 = split2(jnp.where(sub >= lane, corner, 0.0))
+    last = dot(sketch_of(panels - 1), jnp.concatenate([hi, lo16], axis=1), NT)
+    out_ref[:, :top] = acc_ref[:, :top].astype(BF16)
+    out_ref[:, top:] = (acc_ref[:, top:] + last).astype(BF16)
+
+
+def whiten(first, second, sketch):
     width = 2 * first[0].shape[1]
-    panels, rmax, _ = sketch_t.shape
+    panels, rmax = width // NB, sketch.shape[1]
     return pl.pallas_call(
         whiten_kernel,
         out_shape=jax.ShapeDtypeStruct((rmax, width), BF16),
@@ -288,7 +313,7 @@
             pltpu.VMEM((rmax, width), F32),
         ],
         compiler_params=pltpu.CompilerParams(vmem_limit_bytes=24 * 1024 * 1024),
-    )(*first, *second, sketch_t)
+    )(*first, *second, sketch)
 
 
 def basis_kernel(rank_ref, w_ref, sk_ref, turned_ref, basis_ref, first_inv, second_inv):
@@ -347,12 +372,10 @@
 
 def local(calibration, sketch, weights, tile_ranks):
     width = calibration.shape[1]
-    rmax = sketch.shape[1]
     high, low, pieces = prepare(calibration, weights)
     tile_block = lax.all_to_all(pieces, "tile", split_axis=0, concat_axis=0, tiled=True).reshape(width, width)
     first, second = gather_plane(high, low)
-    sketch_t = sketch.reshape(width // NB, NB, rmax).transpose(0, 2, 1)
-    sketched_t = whiten(first, second, sketch_t)
+    sketched_t = whiten(first, second, sketch)
     turned, basis = basis_of(tile_ranks, tile_block, sketched_t)
     served = lax.all_to_all(basis, "tile", split_axis=0, concat_axis=1, tiled=True)
     coeffs = jnp.dot(turned, tile_block, preferred_element_type=F32) / math.sqrt(width)

time: 193 us -> 186 us (0.964)
  local copies, waits for them, and re-layouts: 5.75 us -> 0.85 us
  Pallas kernels: 64.8 us -> 61.9 us
    pallas_call x1, Pallas kernels: 46.9 us -> 44 us  [whiten(): pl.pallas_call(whiten_kernel, out_shape=jax.ShapeDtypeStruct((rmax, width...]
    unnamed x10 -> x6, local copies, waits for them, and re-layouts: 2.88 us -> 0.02 us
    reshape x1 -> x0, local copies, waits for them, and re-layouts: 2.04 us -> none  [local(): sketch_t = sketch.reshape(width // NB, NB, rmax).transpose(0, 2, 1)]
  transfers between devices with their start and end apart: 14 -> 14, of which waited for: 7 -> 7; matrix products, arithmetic and copies ran while one was open for 2% -> 1% of each run, Pallas kernels for 24% -> 24%
where the time goes in v2:
time: 186 us
  starting transfers between devices  75.2 us (40%)
  Pallas kernels  61.9 us (33%)
  waiting for transfers between devices  44.4 us (24%)
    pallas_call x1, Pallas kernels, whiten(): pl.pallas_call(whiten_kernel, out_shape=jax.ShapeDtypeStruct((rmax, width...  44 us
    ppermute x12, starting transfers between devices, shifted(): lax.ppermute(value, axis, [(i, (i + shift) % side) for i in range(side)])  42.6 us
    all_to_all x1, waiting for transfers between devices, local(): lax.all_to_all(basis, 'tile', split_axis=0, concat_axis=1, tiled=True)  32 us
    all_to_all x1, starting transfers between devices, local(): lax.all_to_all(pieces, 'tile', split_axis=0, concat_axis=0, tiled=True)  16.9 us
    all_to_all x1, starting transfers between devices, local(): lax.all_to_all(basis, 'tile', split_axis=0, concat_axis=1, tiled=True)  15.7 us
    pallas_call x1, Pallas kernels, basis_of(): pl.pallas_call(basis_kernel, out_shape=(jax.ShapeDtypeStruct((rmax, width...  13.5 us
    ppermute x12, waiting for transfers between devices, shifted(): lax.ppermute(value, axis, [(i, (i + shift) % side) for i in range(side)])  12.4 us
    pallas_call x1, Pallas kernels, prepare(): pl.pallas_call(prepare_kernel, out_shape=(half, half, jax.ShapeDtypeStruc...  4.38 us
  transfers between devices with their start and end apart: 14, of which 7 were waited for; matrix products, arithmetic and copies ran while one was open for 1% of the time, Pallas kernels for 24%

profile of v2, /device:TPU:1, one launch (start us, length us, event | category | flops | bytes accessed | tf_op | source)
XLA Modules:
  0.0 185.5 jit_solution(13696130423245661706)
XLA Ops:
  0.6 4.4 %shard_map.59 = (bf16[512,128]{1,0:T(8,128)(2,1)}, bf16[512,128]{1,0:T(8,128)(2,1)}, bf16[32,32,1024]{2,1,0:T(8,128)(2,1)}) custom-call(bf16[128,1024]{1,0:T(8,128)(2,1)} %x_ref.1, bf16[32,32768]{1,0:T(8,128)(2,1)} %w_ref.1), custom_call_target="tpu_custom_call" | custom-call | tf_op jit(solution)/shard_map/pallas_call | solution.py:146
  5.0 0.0 copy-start.1
  5.0 0.0 copy-start.2
  5.0 16.9 %all-to-all-start = ((bf16[32,32,1024]{2,1,0:T(8,128)(2,1)}), bf16[32,32,1024]{2,1,0:T(8,128)(2,1)S(1)}, u32[]{:S(2)}, u32[]{:S(2)}) async-start(bf16[32,32,1024]{2,1,0:T(8,128)(2,1)} %get-tuple-element.15), calls=%async_computation | async-start | bytes 4194304 | tf_op jit(solution)/shard_map/all_to_all | solution.py:376
  21.9 0.0 copy-start
  22.0 4.8 %collective-permute-start = (bf16[512,128]{1,0:T(8,128)(2,1)S(1)}, bf16[512,128]{1,0:T(8,128)(2,1)S(1)}, u32[]{:S(2)}, u32[]{:S(2)}) collective-permute-start(bf16[512,128]{1,0:T(8,128)(2,1)S(1)} %copy-done.1), channel_id=1, source_target_pairs={{0,256},{128,384},{256,0},{384,128},{1,257},{129,385},{257,1},{385... | collective-permute-start | bytes 393224 | tf_op jit(solution)/shard_map/ppermute | solution.py:166
  26.8 2.2 %collective-permute-start.1 = (bf16[512,128]{1,0:T(8,128)(2,1)S(1)}, bf16[512,128]{1,0:T(8,128)(2,1)S(1)}, u32[]{:S(2)}, u32[]{:S(2)}) collective-permute-start(bf16[512,128]{1,0:T(8,128)(2,1)S(1)} %copy-done.1), channel_id=1, source_target_pairs={{0,128},{128,256},{256,384},{384,0},{1,129},{129,257},{257,385},{3... | collective-permute-start | bytes 393224 | tf_op jit(solution)/shard_map/ppermute | solution.py:166
  29.0 4.3 %collective-permute-start.2 = (bf16[512,128]{1,0:T(8,128)(2,1)S(1)}, bf16[512,128]{1,0:T(8,128)(2,1)S(1)}, u32[]{:S(2)}, u32[]{:S(2)}) collective-permute-start(bf16[512,128]{1,0:T(8,128)(2,1)S(1)} %copy-done.1), channel_id=1, source_target_pairs={{0,384},{128,0},{256,128},{384,256},{1,385},{129,1},{257,129},{385... | collective-permute-start | bytes 393224 | tf_op jit(solution)/shard_map/ppermute | solution.py:166
  33.3 4.8 %collective-permute-start.3 = (bf16[512,128]{1,0:T(8,128)(2,1)S(1)}, bf16[512,128]{1,0:T(8,128)(2,1)S(1)}, u32[]{:S(2)}, u32[]{:S(2)}) collective-permute-start(bf16[512,128]{1,0:T(8,128)(2,1)S(1)} %copy-done.2), channel_id=1, source_target_pairs={{0,64},{32,96},{64,0},{96,32},{1,65},{33,97},{65,1},{97,33},{2,66}... | collective-permute-start | bytes 393224 | tf_op jit(solution)/shard_map/ppermute | solution.py:166
  38.1 2.3 %collective-permute-start.4 = (bf16[512,128]{1,0:T(8,128)(2,1)S(1)}, bf16[512,128]{1,0:T(8,128)(2,1)S(1)}, u32[]{:S(2)}, u32[]{:S(2)}) collective-permute-start(bf16[512,128]{1,0:T(8,128)(2,1)S(1)} %copy-done.2), channel_id=1, source_target_pairs={{0,32},{32,64},{64,96},{96,0},{1,33},{33,65},{65,97},{97,1},{2,34}... | collective-permute-start | bytes 393224 | tf_op jit(solution)/shard_map/ppermute | solution.py:166
  40.4 0.0 collective-permute-done
  40.4 4.2 %collective-permute-start.5 = (bf16[512,128]{1,0:T(8,128)(2,1)S(1)}, bf16[512,128]{1,0:T(8,128)(2,1)S(1)}, u32[]{:S(2)}, u32[]{:S(2)}) collective-permute-start(bf16[512,128]{1,0:T(8,128)(2,1)S(1)} %copy-done.2), channel_id=1, source_target_pairs={{0,96},{32,0},{64,32},{96,64},{1,97},{33,1},{65,33},{97,65},{2,98}... | collective-permute-start | bytes 393224 | tf_op jit(solution)/shard_map/ppermute | solution.py:166
  44.7 0.7 collective-permute-done.4
  45.3 1.2 collective-permute-done.5
  46.5 0.1 pad_maximum_fusion.1.refs_4_
  46.6 1.9 %collective-permute-start.7 = (bf16[4,512,128]{2,1,0:T(8,128)(2,1)S(1)}, bf16[4,512,128]{2,1,0:T(8,128)(2,1)S(1)}, u32[]{:S(2)}, u32[]{:S(2)}) collective-permute-start(bf16[4,512,128]{2,1,0:T(8,128)(2,1)S(1)} %pad_maximum_fusion.1.refs_4_), channel_id=1, source_target_pairs={{0,384},{128,0},{256,128},{384,256},{1,385},{129,1},{257,129},{385... | collective-permute-start | bytes 1572872 | tf_op jit(solution)/shard_map/ppermute | solution.py:166
  48.5 0.1 pad_maximum_fusion.refs_0_
  48.6 5.3 %collective-permute-start.6 = (bf16[4,512,128]{2,1,0:T(8,128)(2,1)S(1)}, bf16[4,512,128]{2,1,0:T(8,128)(2,1)S(1)}, u32[]{:S(2)}, u32[]{:S(2)}) collective-permute-start(bf16[4,512,128]{2,1,0:T(8,128)(2,1)S(1)} %pad_maximum_fusion.refs_0_), channel_id=1, source_target_pairs={{0,96},{32,0},{64,32},{96,64},{1,97},{33,1},{65,33},{97,65},{2,98}... | collective-permute-start | bytes 1572872 | tf_op jit(solution)/shard_map/ppermute | solution.py:166
  53.9 3.4 %collective-permute-start.11 = (bf16[4,512,128]{2,1,0:T(8,128)(2,1)S(1)}, bf16[4,512,128]{2,1,0:T(8,128)(2,1)S(1)}, u32[]{:S(2)}, u32[]{:S(2)}) collective-permute-start(bf16[4,512,128]{2,1,0:T(8,128)(2,1)S(1)} %pad_maximum_fusion.1.refs_4_), channel_id=1, source_target_pairs={{0,128},{128,256},{256,384},{384,0},{1,129},{129,257},{257,385},{3... | collective-permute-start | bytes 1572872 | tf_op jit(solution)/shard_map/ppermute | solution.py:166
  57.3 1.9 %collective-permute-start.9 = (bf16[4,512,128]{2,1,0:T(8,128)(2,1)S(1)}, bf16[4,512,128]{2,1,0:T(8,128)(2,1)S(1)}, u32[]{:S(2)}, u32[]{:S(2)}) collective-permute-start(bf16[4,512,128]{2,1,0:T(8,128)(2,1)S(1)} %pad_maximum_fusion.refs_0_), channel_id=1, source_target_pairs={{0,32},{32,64},{64,96},{96,0},{1,33},{33,65},{65,97},{97,1},{2,34}... | collective-permute-start | bytes 1572872 | tf_op jit(solution)/shard_map/ppermute | solution.py:166
  59.2 0.2 collective-permute-done.7.refs_7_
  59.4 3.2 %collective-permute-done.6.refs_3_ = bf16[4,512,128]{2,1,0:T(8,128)(2,1)S(1)} collective-permute-done((bf16[4,512,128]{2,1,0:T(8,128)(2,1)S(1)}, bf16[4,512,128]{2,1,0:T(8,128)(2,1)S(1)}, u32[]{:S(2)}, u32[]{:S(2)}) %collective-permute-start.6) | collective-permute-done | bytes 524320 | tf_op jit(solution)/shard_map/ppermute | solution.py:166
  62.6 2.2 %collective-permute-start.10 = (bf16[4,512,128]{2,1,0:T(8,128)(2,1)S(1)}, bf16[4,512,128]{2,1,0:T(8,128)(2,1)S(1)}, u32[]{:S(2)}, u32[]{:S(2)}) collective-permute-start(bf16[4,512,128]{2,1,0:T(8,128)(2,1)S(1)} %collective-permute-done.7.refs_7_), channel_id=1, source_target_pairs={{0,384},{128,0},{256,128},{384,256},{1,385},{129,1},{257,129},{385... | collective-permute-start | bytes 1572872 | tf_op jit(solution)/shard_map/ppermute | solution.py:166
  64.8 5.3 %collective-permute-start.8 = (bf16[4,512,128]{2,1,0:T(8,128)(2,1)S(1)}, bf16[4,512,128]{2,1,0:T(8,128)(2,1)S(1)}, u32[]{:S(2)}, u32[]{:S(2)}) collective-permute-start(bf16[4,512,128]{2,1,0:T(8,128)(2,1)S(1)} %collective-permute-done.6.refs_3_), channel_id=1, source_target_pairs={{0,96},{32,0},{64,32},{96,64},{1,97},{33,1},{65,33},{97,65},{2,98}... | collective-permute-start | bytes 1572872 | tf_op jit(solution)/shard_map/ppermute | solution.py:166
  70.8 3.7 %collective-permute-done.10.refs_5_ = bf16[4,512,128]{2,1,0:T(8,128)(2,1)S(1)} collective-permute-done((bf16[4,512,128]{2,1,0:T(8,128)(2,1)S(1)}, bf16[4,512,128]{2,1,0:T(8,128)(2,1)S(1)}, u32[]{:S(2)}, u32[]{:S(2)}) %collective-permute-start.10) | collective-permute-done | bytes 524320 | tf_op jit(solution)/shard_map/ppermute | solution.py:166
  74.5 3.4 %collective-permute-done.8.refs_1_ = bf16[4,512,128]{2,1,0:T(8,128)(2,1)S(1)} collective-permute-done((bf16[4,512,128]{2,1,0:T(8,128)(2,1)S(1)}, bf16[4,512,128]{2,1,0:T(8,128)(2,1)S(1)}, u32[]{:S(2)}, u32[]{:S(2)}) %collective-permute-start.8) | collective-permute-done | bytes 524320 | tf_op jit(solution)/shard_map/ppermute | solution.py:166
  77.9 44.0 %shard_map.60.sk_ref = bf16[256,1024]{1,0:T(8,128)(2,1)S(1)} custom-call(bf16[4,512,128]{2,1,0:T(8,128)(2,1)S(1)} %pad_maximum_fusion.refs_0_, bf16[4,512,128]{2,1,0:T(8,128)(2,1)S(1)} %collective-permute-done.8.refs_1_, bf16[4,512,128]{2,1,0:T(8,128)(2,1)S(1)} %collective-permute-done.9.refs_2_, bf16[4,512,128]{2,1,0:T(8,128)(2,1)S(1)} %collective-permute-done.6.refs_3_, ...), custom_call_target="tpu_custom_call" | custom-call | tf_op jit(solution)/shard_map/pallas_call | solution.py:304
  121.9 13.5 %shard_map.61 = (bf16[256,1024]{1,0:T(8,128)(2,1)S(1)}, bf16[1024,256]{1,0:T(8,128)(2,1)}) custom-call(s32[1,1]{1,0:T(1,128)S(6)} %copy.8.rank_ref, bf16[1024,1024]{1,0:T(8,128)(2,1)S(1)} %bitcast.15, bf16[256,1024]{1,0:T(8,128)(2,1)S(1)} %shard_map.60.sk_ref), custom_call_target="tpu_custom_call" | custom-call | tf_op jit(solution)/shard_map/pallas_call | solution.py:353
  135.4 15.7 %all-to-all-start.1 = ((bf16[32,32,256]{2,1,0:T(8,128)(2,1)}), bf16[32,32,256]{2,1,0:T(8,128)(2,1)S(1)}, u32[]{:S(2)}, u32[]{:S(2)}) async-start(bf16[32,32,256]{2,1,0:T(8,128)(2,1)} %bitcast.9), calls=%async_computation.1 | async-start | bytes 1048576 | tf_op jit(solution)/shard_map/all_to_all | solution.py:380
  151.2 1.5 fusion
  152.7 32.0 %all-to-all-done.1 = bf16[32,32,256]{2,1,0:T(8,128)(2,1)S(1)} async-done(((bf16[32,32,256]{2,1,0:T(8,128)(2,1)}), bf16[32,32,256]{2,1,0:T(8,128)(2,1)S(1)}, u32[]{:S(2)}, u32[]{:S(2)}) %all-to-all-start.1) | async-done | bytes 524320 | tf_op jit(solution)/shard_map/all_to_all | solution.py:380
  184.7 0.8 copy.7
  (9 shorter events, 0.0 us)
Async XLA Ops:
  5.0 16.9 %copy-start.1 = (bf16[512,128]{1,0:T(8,128)(2,1)S(1)}, bf16[512,128]{1,0:T(8,128)(2,1)}, u32[]{:S(2)}) copy-start(bf16[512,128]{1,0:T(8,128)(2,1)} %get-tuple-element.16) | copy-start | bytes 393220
  5.0 28.2 %copy-start.2 = (bf16[512,128]{1,0:T(8,128)(2,1)S(1)}, bf16[512,128]{1,0:T(8,128)(2,1)}, u32[]{:S(2)}) copy-start(bf16[512,128]{1,0:T(8,128)(2,1)} %get-tuple-element.17) | copy-start | bytes 393220
  5.0 116.9 %all-to-all-start = ((bf16[32,32,1024]{2,1,0:T(8,128)(2,1)}), bf16[32,32,1024]{2,1,0:T(8,128)(2,1)S(1)}, u32[]{:S(2)}, u32[]{:S(2)}) async-start(bf16[32,32,1024]{2,1,0:T(8,128)(2,1)} %get-tuple-element.15), calls=%async_computation | async-start | bytes 4194304 | tf_op jit(solution)/shard_map/all_to_all | solution.py:376
  21.9 56.0 %copy-start = (bf16[1024,256]{1,0:T(8,128)(2,1)S(1)}, bf16[1024,256]{1,0:T(8,128)(2,1)}, u32[]{:S(2)}) copy-start(bf16[1024,256]{1,0:T(8,128)(2,1)} %refs_8_.1) | copy-start | bytes 1572868
  22.0 18.5 %collective-permute-start = (bf16[512,128]{1,0:T(8,128)(2,1)S(1)}, bf16[512,128]{1,0:T(8,128)(2,1)S(1)}, u32[]{:S(2)}, u32[]{:S(2)}) collective-permute-start(bf16[512,128]{1,0:T(8,128)(2,1)S(1)} %copy-done.1), channel_id=1, source_target_pairs={{0,256},{128,384},{256,0},{384,128},{1,257},{129,385},{257,1},{385... | collective-permute-start | bytes 393224 | tf_op jit(solution)/shard_map/ppermute | solution.py:166
  26.8 17.9 %collective-permute-start.1 = (bf16[512,128]{1,0:T(8,128)(2,1)S(1)}, bf16[512,128]{1,0:T(8,128)(2,1)S(1)}, u32[]{:S(2)}, u32[]{:S(2)}) collective-permute-start(bf16[512,128]{1,0:T(8,128)(2,1)S(1)} %copy-done.1), channel_id=1, source_target_pairs={{0,128},{128,256},{256,384},{384,0},{1,129},{129,257},{257,385},{3... | collective-permute-start | bytes 393224 | tf_op jit(solution)/shard_map/ppermute | solution.py:166
  29.0 15.7 %collective-permute-start.2 = (bf16[512,128]{1,0:T(8,128)(2,1)S(1)}, bf16[512,128]{1,0:T(8,128)(2,1)S(1)}, u32[]{:S(2)}, u32[]{:S(2)}) collective-permute-start(bf16[512,128]{1,0:T(8,128)(2,1)S(1)} %copy-done.1), channel_id=1, source_target_pairs={{0,384},{128,0},{256,128},{384,256},{1,385},{129,1},{257,129},{385... | collective-permute-start | bytes 393224 | tf_op jit(solution)/shard_map/ppermute | solution.py:166
  33.3 11.4 %collective-permute-start.3 = (bf16[512,128]{1,0:T(8,128)(2,1)S(1)}, bf16[512,128]{1,0:T(8,128)(2,1)S(1)}, u32[]{:S(2)}, u32[]{:S(2)}) collective-permute-start(bf16[512,128]{1,0:T(8,128)(2,1)S(1)} %copy-done.2), channel_id=1, source_target_pairs={{0,64},{32,96},{64,0},{96,32},{1,65},{33,97},{65,1},{97,33},{2,66}... | collective-permute-start | bytes 393224 | tf_op jit(solution)/shard_map/ppermute | solution.py:166
  38.1 7.2 %collective-permute-start.4 = (bf16[512,128]{1,0:T(8,128)(2,1)S(1)}, bf16[512,128]{1,0:T(8,128)(2,1)S(1)}, u32[]{:S(2)}, u32[]{:S(2)}) collective-permute-start(bf16[512,128]{1,0:T(8,128)(2,1)S(1)} %copy-done.2), channel_id=1, source_target_pairs={{0,32},{32,64},{64,96},{96,0},{1,33},{33,65},{65,97},{97,1},{2,34}... | collective-permute-start | bytes 393224 | tf_op jit(solution)/shard_map/ppermute | solution.py:166
  40.4 6.1 %collective-permute-start.5 = (bf16[512,128]{1,0:T(8,128)(2,1)S(1)}, bf16[512,128]{1,0:T(8,128)(2,1)S(1)}, u32[]{:S(2)}, u32[]{:S(2)}) collective-permute-start(bf16[512,128]{1,0:T(8,128)(2,1)S(1)} %copy-done.2), channel_id=1, source_target_pairs={{0,96},{32,0},{64,32},{96,64},{1,97},{33,1},{65,33},{97,65},{2,98}... | collective-permute-start | bytes 393224 | tf_op jit(solution)/shard_map/ppermute | solution.py:166
  46.6 12.8 %collective-permute-start.7 = (bf16[4,512,128]{2,1,0:T(8,128)(2,1)S(1)}, bf16[4,512,128]{2,1,0:T(8,128)(2,1)S(1)}, u32[]{:S(2)}, u32[]{:S(2)}) collective-permute-start(bf16[4,512,128]{2,1,0:T(8,128)(2,1)S(1)} %pad_maximum_fusion.1.refs_4_), channel_id=1, source_target_pairs={{0,384},{128,0},{256,128},{384,256},{1,385},{129,1},{257,129},{385... | collective-permute-start | bytes 1572872 | tf_op jit(solution)/shard_map/ppermute | solution.py:166
  48.6 14.0 %collective-permute-start.6 = (bf16[4,512,128]{2,1,0:T(8,128)(2,1)S(1)}, bf16[4,512,128]{2,1,0:T(8,128)(2,1)S(1)}, u32[]{:S(2)}, u32[]{:S(2)}) collective-permute-start(bf16[4,512,128]{2,1,0:T(8,128)(2,1)S(1)} %pad_maximum_fusion.refs_0_), channel_id=1, source_target_pairs={{0,96},{32,0},{64,32},{96,64},{1,97},{33,1},{65,33},{97,65},{2,98}... | collective-permute-start | bytes 1572872 | tf_op jit(solution)/shard_map/ppermute | solution.py:166
  53.9 16.9 %collective-permute-start.11 = (bf16[4,512,128]{2,1,0:T(8,128)(2,1)S(1)}, bf16[4,512,128]{2,1,0:T(8,128)(2,1)S(1)}, u32[]{:S(2)}, u32[]{:S(2)}) collective-permute-start(bf16[4,512,128]{2,1,0:T(8,128)(2,1)S(1)} %pad_maximum_fusion.1.refs_4_), channel_id=1, source_target_pairs={{0,128},{128,256},{256,384},{384,0},{1,129},{129,257},{257,385},{3... | collective-permute-start | bytes 1572872 | tf_op jit(solution)/shard_map/ppermute | solution.py:166
  57.3 13.5 %collective-permute-start.9 = (bf16[4,512,128]{2,1,0:T(8,128)(2,1)S(1)}, bf16[4,512,128]{2,1,0:T(8,128)(2,1)S(1)}, u32[]{:S(2)}, u32[]{:S(2)}) collective-permute-start(bf16[4,512,128]{2,1,0:T(8,128)(2,1)S(1)} %pad_maximum_fusion.refs_0_), channel_id=1, source_target_pairs={{0,32},{32,64},{64,96},{96,0},{1,33},{33,65},{65,97},{97,1},{2,34}... | collective-permute-start | bytes 1572872 | tf_op jit(solution)/shard_map/ppermute | solution.py:166
  62.6 11.9 %collective-permute-start.10 = (bf16[4,512,128]{2,1,0:T(8,128)(2,1)S(1)}, bf16[4,512,128]{2,1,0:T(8,128)(2,1)S(1)}, u32[]{:S(2)}, u32[]{:S(2)}) collective-permute-start(bf16[4,512,128]{2,1,0:T(8,128)(2,1)S(1)} %collective-permute-done.7.refs_7_), channel_id=1, source_target_pairs={{0,384},{128,0},{256,128},{384,256},{1,385},{129,1},{257,129},{385... | collective-permute-start | bytes 1572872 | tf_op jit(solution)/shard_map/ppermute | solution.py:166
  64.8 13.1 %collective-permute-start.8 = (bf16[4,512,128]{2,1,0:T(8,128)(2,1)S(1)}, bf16[4,512,128]{2,1,0:T(8,128)(2,1)S(1)}, u32[]{:S(2)}, u32[]{:S(2)}) collective-permute-start(bf16[4,512,128]{2,1,0:T(8,128)(2,1)S(1)} %collective-permute-done.6.refs_3_), channel_id=1, source_target_pairs={{0,96},{32,0},{64,32},{96,64},{1,97},{33,1},{65,33},{97,65},{2,98}... | collective-permute-start | bytes 1572872 | tf_op jit(solution)/shard_map/ppermute | solution.py:166
  135.4 49.3 %all-to-all-start.1 = ((bf16[32,32,256]{2,1,0:T(8,128)(2,1)}), bf16[32,32,256]{2,1,0:T(8,128)(2,1)S(1)}, u32[]{:S(2)}, u32[]{:S(2)}) async-start(bf16[32,32,256]{2,1,0:T(8,128)(2,1)} %bitcast.9), calls=%async_computation.1 | async-start | bytes 1048576 | tf_op jit(solution)/shard_map/all_to_all | solution.py:380

commit v3 on v2

--- a/solution.py
+++ b/solution.py
@@ -115,7 +115,7 @@
         inv_ref[s * STRIP : (s + 1) * STRIP, :] = rows
 
 
-def prepare_kernel(x_ref, w_ref, high_ref, low_ref, pieces_ref, hold_ref, in_sems, out_sems):
+def prepare_kernel(x_ref, w_ref, high_ref, low_ref, pieces_ref, hold_ref, x_hold, turned, in_sems, out_sems, x_sems):
     pieces, _, width = hold_ref.shape
     group = pieces // PREPARE_STEPS
     inward = [
@@ -125,16 +125,22 @@
         pltpu.make_async_copy(hold_ref.at[pl.ds(g * group, group)], pieces_ref.at[pl.ds(g * group, group)], out_sems.at[g])
         for g in range(PREPARE_STEPS)
     ]
+    load = pltpu.make_async_copy(x_ref, x_hold, x_sems.at[2])
+    load.start()
     for copy in inward:
         copy.start()
+    load.wait()
     half = high_ref.shape[0]
-    high_ref[...] = x_ref[:, :half].T
-    low_ref[...] = x_ref[:, half:].T
+    stores = []
+    for i, ref in enumerate((high_ref, low_ref)):
+        turned[i] = x_hold[:, i * half : (i + 1) * half].T
+        stores.append(pltpu.make_async_copy(turned.at[i], ref, x_sems.at[i]))
+        stores[i].start()
     for g in range(PREPARE_STEPS):
         for copy in inward[g * group : (g + 1) * group]:
             copy.wait()
         outward[g].start()
-    for copy in outward:
+    for copy in outward + stores:
         copy.wait()
 
 
@@ -146,16 +152,15 @@
     return pl.pallas_call(
         prepare_kernel,
         out_shape=(half, half, jax.ShapeDtypeStruct((pieces, rows, width), weights.dtype)),
-        in_specs=[pl.BlockSpec(memory_space=pltpu.VMEM), pl.BlockSpec(memory_space=pl.ANY)],
-        out_specs=(
-            pl.BlockSpec(memory_space=pltpu.VMEM),
-            pl.BlockSpec(memory_space=pltpu.VMEM),
-            pl.BlockSpec(memory_space=pl.ANY),
-        ),
+        in_specs=[pl.BlockSpec(memory_space=pl.ANY)] * 2,
+        out_specs=(pl.BlockSpec(memory_space=pl.ANY),) * 3,
         scratch_shapes=[
             pltpu.VMEM((pieces, rows, width), weights.dtype),
+            pltpu.VMEM((tokens, width), x.dtype),
+            pltpu.VMEM((2, width // 2, tokens), x.dtype),
             pltpu.SemaphoreType.DMA((pieces,)),
             pltpu.SemaphoreType.DMA((PREPARE_STEPS,)),
+            pltpu.SemaphoreType.DMA((3,)),
         ],
         compiler_params=pltpu.CompilerParams(vmem_limit_bytes=GRANT),
     )(x, weights)

time: 186 us -> 185 us (level)
  no operation moved by 1% of the time
where the time goes in v3:
time: 185 us
  starting transfers between devices  75.2 us (41%)
  Pallas kernels  61 us (33%)
  waiting for transfers between devices  44.4 us (24%)
    pallas_call x1, Pallas kernels, whiten(): pl.pallas_call(whiten_kernel, out_shape=jax.ShapeDtypeStruct((rmax, width...  44 us
    ppermute x12, starting transfers between devices, shifted(): lax.ppermute(value, axis, [(i, (i + shift) % side) for i in range(side)])  42.6 us
    all_to_all x1, waiting for transfers between devices, local(): lax.all_to_all(basis, 'tile', split_axis=0, concat_axis=1, tiled=True)  32 us
    all_to_all x1, starting transfers between devices, local(): lax.all_to_all(pieces, 'tile', split_axis=0, concat_axis=0, tiled=True)  16.9 us
    all_to_all x1, starting transfers between devices, local(): lax.all_to_all(basis, 'tile', split_axis=0, concat_axis=1, tiled=True)  15.7 us
    pallas_call x1, Pallas kernels, basis_of(): pl.pallas_call(basis_kernel, out_shape=(jax.ShapeDtypeStruct((rmax, width...  13.5 us
    ppermute x12, waiting for transfers between devices, shifted(): lax.ppermute(value, axis, [(i, (i + shift) % side) for i in range(side)])  12.4 us
  transfers between devices with their start and end apart: 14, of which 7 were waited for; matrix products, arithmetic and copies ran while one was open for 1% of the time, Pallas kernels for 24%

profile of v3, /device:TPU:1, one launch (start us, length us, event | category | flops | bytes accessed | tf_op | source)
XLA Modules:
  0.0 184.7 jit_solution(4147397527791257490)
XLA Ops:
  0.6 3.6 %shard_map.59 = (bf16[512,128]{1,0:T(8,128)(2,1)}, bf16[512,128]{1,0:T(8,128)(2,1)}, bf16[32,32,1024]{2,1,0:T(8,128)(2,1)}) custom-call(bf16[128,1024]{1,0:T(8,128)(2,1)} %x_ref.1, bf16[32,32768]{1,0:T(8,128)(2,1)} %w_ref.1), custom_call_target="tpu_custom_call" | custom-call | tf_op jit(solution)/shard_map/pallas_call | solution.py:152
  4.2 0.0 copy-start.1
  4.2 0.0 copy-start.2
  4.2 16.9 %all-to-all-start = ((bf16[32,32,1024]{2,1,0:T(8,128)(2,1)}), bf16[32,32,1024]{2,1,0:T(8,128)(2,1)S(1)}, u32[]{:S(2)}, u32[]{:S(2)}) async-start(bf16[32,32,1024]{2,1,0:T(8,128)(2,1)} %get-tuple-element.15), calls=%async_computation | async-start | bytes 4194304 | tf_op jit(solution)/shard_map/all_to_all | solution.py:381
  21.1 0.0 copy-start
  21.1 4.8 %collective-permute-start = (bf16[512,128]{1,0:T(8,128)(2,1)S(1)}, bf16[512,128]{1,0:T(8,128)(2,1)S(1)}, u32[]{:S(2)}, u32[]{:S(2)}) collective-permute-start(bf16[512,128]{1,0:T(8,128)(2,1)S(1)} %copy-done.1), channel_id=1, source_target_pairs={{0,256},{128,384},{256,0},{384,128},{1,257},{129,385},{257,1},{385... | collective-permute-start | bytes 393224 | tf_op jit(solution)/shard_map/ppermute | solution.py:171
  25.9 2.2 %collective-permute-start.1 = (bf16[512,128]{1,0:T(8,128)(2,1)S(1)}, bf16[512,128]{1,0:T(8,128)(2,1)S(1)}, u32[]{:S(2)}, u32[]{:S(2)}) collective-permute-start(bf16[512,128]{1,0:T(8,128)(2,1)S(1)} %copy-done.1), channel_id=1, source_target_pairs={{0,128},{128,256},{256,384},{384,0},{1,129},{129,257},{257,385},{3... | collective-permute-start | bytes 393224 | tf_op jit(solution)/shard_map/ppermute | solution.py:171
  28.2 4.3 %collective-permute-start.2 = (bf16[512,128]{1,0:T(8,128)(2,1)S(1)}, bf16[512,128]{1,0:T(8,128)(2,1)S(1)}, u32[]{:S(2)}, u32[]{:S(2)}) collective-permute-start(bf16[512,128]{1,0:T(8,128)(2,1)S(1)} %copy-done.1), channel_id=1, source_target_pairs={{0,384},{128,0},{256,128},{384,256},{1,385},{129,1},{257,129},{385... | collective-permute-start | bytes 393224 | tf_op jit(solution)/shard_map/ppermute | solution.py:171
  32.4 4.8 %collective-permute-start.3 = (bf16[512,128]{1,0:T(8,128)(2,1)S(1)}, bf16[512,128]{1,0:T(8,128)(2,1)S(1)}, u32[]{:S(2)}, u32[]{:S(2)}) collective-permute-start(bf16[512,128]{1,0:T(8,128)(2,1)S(1)} %copy-done.2), channel_id=1, source_target_pairs={{0,64},{32,96},{64,0},{96,32},{1,65},{33,97},{65,1},{97,33},{2,66}... | collective-permute-start | bytes 393224 | tf_op jit(solution)/shard_map/ppermute | solution.py:171
  37.3 2.3 %collective-permute-start.4 = (bf16[512,128]{1,0:T(8,128)(2,1)S(1)}, bf16[512,128]{1,0:T(8,128)(2,1)S(1)}, u32[]{:S(2)}, u32[]{:S(2)}) collective-permute-start(bf16[512,128]{1,0:T(8,128)(2,1)S(1)} %copy-done.2), channel_id=1, source_target_pairs={{0,32},{32,64},{64,96},{96,0},{1,33},{33,65},{65,97},{97,1},{2,34}... | collective-permute-start | bytes 393224 | tf_op jit(solution)/shard_map/ppermute | solution.py:171
  39.6 0.0 collective-permute-done
  39.6 4.2 %collective-permute-start.5 = (bf16[512,128]{1,0:T(8,128)(2,1)S(1)}, bf16[512,128]{1,0:T(8,128)(2,1)S(1)}, u32[]{:S(2)}, u32[]{:S(2)}) collective-permute-start(bf16[512,128]{1,0:T(8,128)(2,1)S(1)} %copy-done.2), channel_id=1, source_target_pairs={{0,96},{32,0},{64,32},{96,64},{1,97},{33,1},{65,33},{97,65},{2,98}... | collective-permute-start | bytes 393224 | tf_op jit(solution)/shard_map/ppermute | solution.py:171
  43.8 0.7 collective-permute-done.4
  44.5 1.2 collective-permute-done.5
  45.7 0.1 pad_maximum_fusion.1.refs_4_
  45.8 1.9 %collective-permute-start.7 = (bf16[4,512,128]{2,1,0:T(8,128)(2,1)S(1)}, bf16[4,512,128]{2,1,0:T(8,128)(2,1)S(1)}, u32[]{:S(2)}, u32[]{:S(2)}) collective-permute-start(bf16[4,512,128]{2,1,0:T(8,128)(2,1)S(1)} %pad_maximum_fusion.1.refs_4_), channel_id=1, source_target_pairs={{0,384},{128,0},{256,128},{384,256},{1,385},{129,1},{257,129},{385... | collective-permute-start | bytes 1572872 | tf_op jit(solution)/shard_map/ppermute | solution.py:171
  47.7 0.1 pad_maximum_fusion.refs_0_
  47.8 5.3 %collective-permute-start.6 = (bf16[4,512,128]{2,1,0:T(8,128)(2,1)S(1)}, bf16[4,512,128]{2,1,0:T(8,128)(2,1)S(1)}, u32[]{:S(2)}, u32[]{:S(2)}) collective-permute-start(bf16[4,512,128]{2,1,0:T(8,128)(2,1)S(1)} %pad_maximum_fusion.refs_0_), channel_id=1, source_target_pairs={{0,96},{32,0},{64,32},{96,64},{1,97},{33,1},{65,33},{97,65},{2,98}... | collective-permute-start | bytes 1572872 | tf_op jit(solution)/shard_map/ppermute | solution.py:171
  53.1 3.4 %collective-permute-start.11 = (bf16[4,512,128]{2,1,0:T(8,128)(2,1)S(1)}, bf16[4,512,128]{2,1,0:T(8,128)(2,1)S(1)}, u32[]{:S(2)}, u32[]{:S(2)}) collective-permute-start(bf16[4,512,128]{2,1,0:T(8,128)(2,1)S(1)} %pad_maximum_fusion.1.refs_4_), channel_id=1, source_target_pairs={{0,128},{128,256},{256,384},{384,0},{1,129},{129,257},{257,385},{3... | collective-permute-start | bytes 1572872 | tf_op jit(solution)/shard_map/ppermute | solution.py:171
  56.5 1.9 %collective-permute-start.9 = (bf16[4,512,128]{2,1,0:T(8,128)(2,1)S(1)}, bf16[4,512,128]{2,1,0:T(8,128)(2,1)S(1)}, u32[]{:S(2)}, u32[]{:S(2)}) collective-permute-start(bf16[4,512,128]{2,1,0:T(8,128)(2,1)S(1)} %pad_maximum_fusion.refs_0_), channel_id=1, source_target_pairs={{0,32},{32,64},{64,96},{96,0},{1,33},{33,65},{65,97},{97,1},{2,34}... | collective-permute-start | bytes 1572872 | tf_op jit(solution)/shard_map/ppermute | solution.py:171
  58.4 0.2 collective-permute-done.7.refs_7_
  58.6 3.2 %collective-permute-done.6.refs_3_ = bf16[4,512,128]{2,1,0:T(8,128)(2,1)S(1)} collective-permute-done((bf16[4,512,128]{2,1,0:T(8,128)(2,1)S(1)}, bf16[4,512,128]{2,1,0:T(8,128)(2,1)S(1)}, u32[]{:S(2)}, u32[]{:S(2)}) %collective-permute-start.6) | collective-permute-done | bytes 524320 | tf_op jit(solution)/shard_map/ppermute | solution.py:171
  61.8 2.2 %collective-permute-start.10 = (bf16[4,512,128]{2,1,0:T(8,128)(2,1)S(1)}, bf16[4,512,128]{2,1,0:T(8,128)(2,1)S(1)}, u32[]{:S(2)}, u32[]{:S(2)}) collective-permute-start(bf16[4,512,128]{2,1,0:T(8,128)(2,1)S(1)} %collective-permute-done.7.refs_7_), channel_id=1, source_target_pairs={{0,384},{128,0},{256,128},{384,256},{1,385},{129,1},{257,129},{385... | collective-permute-start | bytes 1572872 | tf_op jit(solution)/shard_map/ppermute | solution.py:171
  64.0 5.3 %collective-permute-start.8 = (bf16[4,512,128]{2,1,0:T(8,128)(2,1)S(1)}, bf16[4,512,128]{2,1,0:T(8,128)(2,1)S(1)}, u32[]{:S(2)}, u32[]{:S(2)}) collective-permute-start(bf16[4,512,128]{2,1,0:T(8,128)(2,1)S(1)} %collective-permute-done.6.refs_3_), channel_id=1, source_target_pairs={{0,96},{32,0},{64,32},{96,64},{1,97},{33,1},{65,33},{97,65},{2,98}... | collective-permute-start | bytes 1572872 | tf_op jit(solution)/shard_map/ppermute | solution.py:171
  70.0 3.7 %collective-permute-done.10.refs_5_ = bf16[4,512,128]{2,1,0:T(8,128)(2,1)S(1)} collective-permute-done((bf16[4,512,128]{2,1,0:T(8,128)(2,1)S(1)}, bf16[4,512,128]{2,1,0:T(8,128)(2,1)S(1)}, u32[]{:S(2)}, u32[]{:S(2)}) %collective-permute-start.10) | collective-permute-done | bytes 524320 | tf_op jit(solution)/shard_map/ppermute | solution.py:171
  73.7 3.4 %collective-permute-done.8.refs_1_ = bf16[4,512,128]{2,1,0:T(8,128)(2,1)S(1)} collective-permute-done((bf16[4,512,128]{2,1,0:T(8,128)(2,1)S(1)}, bf16[4,512,128]{2,1,0:T(8,128)(2,1)S(1)}, u32[]{:S(2)}, u32[]{:S(2)}) %collective-permute-start.8) | collective-permute-done | bytes 524320 | tf_op jit(solution)/shard_map/ppermute | solution.py:171
  77.1 44.0 %shard_map.60.sk_ref = bf16[256,1024]{1,0:T(8,128)(2,1)S(1)} custom-call(bf16[4,512,128]{2,1,0:T(8,128)(2,1)S(1)} %pad_maximum_fusion.refs_0_, bf16[4,512,128]{2,1,0:T(8,128)(2,1)S(1)} %collective-permute-done.8.refs_1_, bf16[4,512,128]{2,1,0:T(8,128)(2,1)S(1)} %collective-permute-done.9.refs_2_, bf16[4,512,128]{2,1,0:T(8,128)(2,1)S(1)} %collective-permute-done.6.refs_3_, ...), custom_call_target="tpu_custom_call" | custom-call | tf_op jit(solution)/shard_map/pallas_call | solution.py:309
  121.1 13.5 %shard_map.61 = (bf16[256,1024]{1,0:T(8,128)(2,1)S(1)}, bf16[1024,256]{1,0:T(8,128)(2,1)}) custom-call(s32[1,1]{1,0:T(1,128)S(6)} %copy.8.rank_ref, bf16[1024,1024]{1,0:T(8,128)(2,1)S(1)} %bitcast.15, bf16[256,1024]{1,0:T(8,128)(2,1)S(1)} %shard_map.60.sk_ref), custom_call_target="tpu_custom_call" | custom-call | tf_op jit(solution)/shard_map/pallas_call | solution.py:358
  134.6 15.7 %all-to-all-start.1 = ((bf16[32,32,256]{2,1,0:T(8,128)(2,1)}), bf16[32,32,256]{2,1,0:T(8,128)(2,1)S(1)}, u32[]{:S(2)}, u32[]{:S(2)}) async-start(bf16[32,32,256]{2,1,0:T(8,128)(2,1)} %bitcast.9), calls=%async_computation.1 | async-start | bytes 1048576 | tf_op jit(solution)/shard_map/all_to_all | solution.py:385
  150.4 1.5 fusion
  151.9 32.0 %all-to-all-done.1 = bf16[32,32,256]{2,1,0:T(8,128)(2,1)S(1)} async-done(((bf16[32,32,256]{2,1,0:T(8,128)(2,1)}), bf16[32,32,256]{2,1,0:T(8,128)(2,1)S(1)}, u32[]{:S(2)}, u32[]{:S(2)}) %all-to-all-start.1) | async-done | bytes 524320 | tf_op jit(solution)/shard_map/all_to_all | solution.py:385
  183.9 0.8 copy.7
  (9 shorter events, 0.0 us)
Async XLA Ops:
  4.2 16.9 %copy-start.1 = (bf16[512,128]{1,0:T(8,128)(2,1)S(1)}, bf16[512,128]{1,0:T(8,128)(2,1)}, u32[]{:S(2)}) copy-start(bf16[512,128]{1,0:T(8,128)(2,1)} %get-tuple-element.16) | copy-start | bytes 393220
  4.2 28.2 %copy-start.2 = (bf16[512,128]{1,0:T(8,128)(2,1)S(1)}, bf16[512,128]{1,0:T(8,128)(2,1)}, u32[]{:S(2)}) copy-start(bf16[512,128]{1,0:T(8,128)(2,1)} %get-tuple-element.17) | copy-start | bytes 393220
  4.2 116.9 %all-to-all-start = ((bf16[32,32,1024]{2,1,0:T(8,128)(2,1)}), bf16[32,32,1024]{2,1,0:T(8,128)(2,1)S(1)}, u32[]{:S(2)}, u32[]{:S(2)}) async-start(bf16[32,32,1024]{2,1,0:T(8,128)(2,1)} %get-tuple-element.15), calls=%async_computation | async-start | bytes 4194304 | tf_op jit(solution)/shard_map/all_to_all | solution.py:381
  21.1 56.0 %copy-start = (bf16[1024,256]{1,0:T(8,128)(2,1)S(1)}, bf16[1024,256]{1,0:T(8,128)(2,1)}, u32[]{:S(2)}) copy-start(bf16[1024,256]{1,0:T(8,128)(2,1)} %refs_8_.1) | copy-start | bytes 1572868
  21.1 18.5 %collective-permute-start = (bf16[512,128]{1,0:T(8,128)(2,1)S(1)}, bf16[512,128]{1,0:T(8,128)(2,1)S(1)}, u32[]{:S(2)}, u32[]{:S(2)}) collective-permute-start(bf16[512,128]{1,0:T(8,128)(2,1)S(1)} %copy-done.1), channel_id=1, source_target_pairs={{0,256},{128,384},{256,0},{384,128},{1,257},{129,385},{257,1},{385... | collective-permute-start | bytes 393224 | tf_op jit(solution)/shard_map/ppermute | solution.py:171
  25.9 17.9 %collective-permute-start.1 = (bf16[512,128]{1,0:T(8,128)(2,1)S(1)}, bf16[512,128]{1,0:T(8,128)(2,1)S(1)}, u32[]{:S(2)}, u32[]{:S(2)}) collective-permute-start(bf16[512,128]{1,0:T(8,128)(2,1)S(1)} %copy-done.1), channel_id=1, source_target_pairs={{0,128},{128,256},{256,384},{384,0},{1,129},{129,257},{257,385},{3... | collective-permute-start | bytes 393224 | tf_op jit(solution)/shard_map/ppermute | solution.py:171
  28.2 15.7 %collective-permute-start.2 = (bf16[512,128]{1,0:T(8,128)(2,1)S(1)}, bf16[512,128]{1,0:T(8,128)(2,1)S(1)}, u32[]{:S(2)}, u32[]{:S(2)}) collective-permute-start(bf16[512,128]{1,0:T(8,128)(2,1)S(1)} %copy-done.1), channel_id=1, source_target_pairs={{0,384},{128,0},{256,128},{384,256},{1,385},{129,1},{257,129},{385... | collective-permute-start | bytes 393224 | tf_op jit(solution)/shard_map/ppermute | solution.py:171
  32.4 11.4 %collective-permute-start.3 = (bf16[512,128]{1,0:T(8,128)(2,1)S(1)}, bf16[512,128]{1,0:T(8,128)(2,1)S(1)}, u32[]{:S(2)}, u32[]{:S(2)}) collective-permute-start(bf16[512,128]{1,0:T(8,128)(2,1)S(1)} %copy-done.2), channel_id=1, source_target_pairs={{0,64},{32,96},{64,0},{96,32},{1,65},{33,97},{65,1},{97,33},{2,66}... | collective-permute-start | bytes 393224 | tf_op jit(solution)/shard_map/ppermute | solution.py:171
  37.3 7.2 %collective-permute-start.4 = (bf16[512,128]{1,0:T(8,128)(2,1)S(1)}, bf16[512,128]{1,0:T(8,128)(2,1)S(1)}, u32[]{:S(2)}, u32[]{:S(2)}) collective-permute-start(bf16[512,128]{1,0:T(8,128)(2,1)S(1)} %copy-done.2), channel_id=1, source_target_pairs={{0,32},{32,64},{64,96},{96,0},{1,33},{33,65},{65,97},{97,1},{2,34}... | collective-permute-start | bytes 393224 | tf_op jit(solution)/shard_map/ppermute | solution.py:171
  39.6 6.1 %collective-permute-start.5 = (bf16[512,128]{1,0:T(8,128)(2,1)S(1)}, bf16[512,128]{1,0:T(8,128)(2,1)S(1)}, u32[]{:S(2)}, u32[]{:S(2)}) collective-permute-start(bf16[512,128]{1,0:T(8,128)(2,1)S(1)} %copy-done.2), channel_id=1, source_target_pairs={{0,96},{32,0},{64,32},{96,64},{1,97},{33,1},{65,33},{97,65},{2,98}... | collective-permute-start | bytes 393224 | tf_op jit(solution)/shard_map/ppermute | solution.py:171
  45.8 12.8 %collective-permute-start.7 = (bf16[4,512,128]{2,1,0:T(8,128)(2,1)S(1)}, bf16[4,512,128]{2,1,0:T(8,128)(2,1)S(1)}, u32[]{:S(2)}, u32[]{:S(2)}) collective-permute-start(bf16[4,512,128]{2,1,0:T(8,128)(2,1)S(1)} %pad_maximum_fusion.1.refs_4_), channel_id=1, source_target_pairs={{0,384},{128,0},{256,128},{384,256},{1,385},{129,1},{257,129},{385... | collective-permute-start | bytes 1572872 | tf_op jit(solution)/shard_map/ppermute | solution.py:171
  47.8 14.0 %collective-permute-start.6 = (bf16[4,512,128]{2,1,0:T(8,128)(2,1)S(1)}, bf16[4,512,128]{2,1,0:T(8,128)(2,1)S(1)}, u32[]{:S(2)}, u32[]{:S(2)}) collective-permute-start(bf16[4,512,128]{2,1,0:T(8,128)(2,1)S(1)} %pad_maximum_fusion.refs_0_), channel_id=1, source_target_pairs={{0,96},{32,0},{64,32},{96,64},{1,97},{33,1},{65,33},{97,65},{2,98}... | collective-permute-start | bytes 1572872 | tf_op jit(solution)/shard_map/ppermute | solution.py:171
  53.1 16.9 %collective-permute-start.11 = (bf16[4,512,128]{2,1,0:T(8,128)(2,1)S(1)}, bf16[4,512,128]{2,1,0:T(8,128)(2,1)S(1)}, u32[]{:S(2)}, u32[]{:S(2)}) collective-permute-start(bf16[4,512,128]{2,1,0:T(8,128)(2,1)S(1)} %pad_maximum_fusion.1.refs_4_), channel_id=1, source_target_pairs={{0,128},{128,256},{256,384},{384,0},{1,129},{129,257},{257,385},{3... | collective-permute-start | bytes 1572872 | tf_op jit(solution)/shard_map/ppermute | solution.py:171
  56.5 13.5 %collective-permute-start.9 = (bf16[4,512,128]{2,1,0:T(8,128)(2,1)S(1)}, bf16[4,512,128]{2,1,0:T(8,128)(2,1)S(1)}, u32[]{:S(2)}, u32[]{:S(2)}) collective-permute-start(bf16[4,512,128]{2,1,0:T(8,128)(2,1)S(1)} %pad_maximum_fusion.refs_0_), channel_id=1, source_target_pairs={{0,32},{32,64},{64,96},{96,0},{1,33},{33,65},{65,97},{97,1},{2,34}... | collective-permute-start | bytes 1572872 | tf_op jit(solution)/shard_map/ppermute | solution.py:171
  61.8 11.9 %collective-permute-start.10 = (bf16[4,512,128]{2,1,0:T(8,128)(2,1)S(1)}, bf16[4,512,128]{2,1,0:T(8,128)(2,1)S(1)}, u32[]{:S(2)}, u32[]{:S(2)}) collective-permute-start(bf16[4,512,128]{2,1,0:T(8,128)(2,1)S(1)} %collective-permute-done.7.refs_7_), channel_id=1, source_target_pairs={{0,384},{128,0},{256,128},{384,256},{1,385},{129,1},{257,129},{385... | collective-permute-start | bytes 1572872 | tf_op jit(solution)/shard_map/ppermute | solution.py:171
  64.0 13.1 %collective-permute-start.8 = (bf16[4,512,128]{2,1,0:T(8,128)(2,1)S(1)}, bf16[4,512,128]{2,1,0:T(8,128)(2,1)S(1)}, u32[]{:S(2)}, u32[]{:S(2)}) collective-permute-start(bf16[4,512,128]{2,1,0:T(8,128)(2,1)S(1)} %collective-permute-done.6.refs_3_), channel_id=1, source_target_pairs={{0,96},{32,0},{64,32},{96,64},{1,97},{33,1},{65,33},{97,65},{2,98}... | collective-permute-start | bytes 1572872 | tf_op jit(solution)/shard_map/ppermute | solution.py:171
  134.6 49.3 %all-to-all-start.1 = ((bf16[32,32,256]{2,1,0:T(8,128)(2,1)}), bf16[32,32,256]{2,1,0:T(8,128)(2,1)S(1)}, u32[]{:S(2)}, u32[]{:S(2)}) async-start(bf16[32,32,256]{2,1,0:T(8,128)(2,1)} %bitcast.9), calls=%async_computation.1 | async-start | bytes 1048576 | tf_op jit(solution)/shard_map/all_to_all | solution.py:385
